TPU v7x, 32 devices: a whole 2x2x4 slice. The times are simulated.
32 devices in a mesh: row: 4 (over y, x), col: 8 (over z, core).
Axes of the slice: x: 2, y: 2, z: 4, core: 2. Of those that a mesh axis runs over, the one named last changes fastest.
Arguments:
- features: bfloat16 [4096, 512], P(('row', 'col')), may hold values from -6 to 6
- adj_tiles: bfloat16 [4, 64, 128, 128], P('row', 'col'), may hold values from -0.1875 to 0.1875
- tile_rows: int32 [4, 64], P('row', 'col'), may hold values from 0 to 7, as said below
- tile_cols: int32 [4, 64], P('row', 'col'), may hold values from 0 to 3
- tile_count: int32 [4, 8], P('row', 'col'), may hold values from 1 to 8, as said below
- weight: bfloat16 [1024, 512], replicated, may hold values from -0.25 to 0.25
- cotangent: bfloat16 [4096, 512], P(('row', 'col')), may hold values from -6 to 6
Outputs:
- hidden: bfloat16 [4096, 512], P(('row', 'col'))
- weight_grad: float32 [1024, 512], replicated
Inputs may be any that keep to these rules, and one draw needn't show every extreme that they name: `tile_count`: some device has all 8 slots live. `tile_rows`: every slot of device (r, c) names tile row (c + k) mod 8 with 0 <= k < 4; slot 0 of every device has k = 3.
All inputs are finite; a program needn't handle non-finite values.
Results may differ from a plain program's by a relative error of at most 0.0035.
Values may be sent and summed in bfloat16 or wider, within the bound.
A program may use at most 64 MiB of HBM per device.

v0:
```python
import jax
import jax.numpy as jnp
from jax import lax
from jax.sharding import PartitionSpec as P

REACH = 4


def from_behind(value, axis, steps):
    count = lax.axis_size(axis)
    pairs = [(source, (source + steps) % count) for source in range(count)]
    return lax.ppermute(value, axis, pairs)


def tile_forward(adj_tiles, rows_idx, cols_idx, count, source, num_rows):
    width = source.shape[1]
    tile_size = adj_tiles.shape[1]
    blocks = source.reshape(-1, tile_size, width)
    chosen = jnp.take(blocks, cols_idx, axis=0)
    products = jnp.einsum("tij,tjx->tix", adj_tiles, chosen, preferred_element_type=jnp.float32)
    live_mask = (jnp.arange(adj_tiles.shape[0]) < count).astype(jnp.float32)
    placing = (rows_idx[:, None] == jnp.arange(num_rows)[None, :]).astype(jnp.float32) * live_mask[
        :, None
    ]
    return jnp.einsum("tr,tix->rix", placing, products, precision=lax.Precision.HIGHEST)


def tile_backward(adj_tiles, rows_idx, cols_idx, count, source, num_cols):
    width = source.shape[1]
    tile_size = adj_tiles.shape[1]
    blocks = source.reshape(-1, tile_size, width)
    chosen = jnp.take(blocks, rows_idx, axis=0)
    products = jnp.einsum("tji,tjx->tix", adj_tiles, chosen, preferred_element_type=jnp.float32)
    live_mask = (jnp.arange(adj_tiles.shape[0]) < count).astype(jnp.float32)
    placing = (cols_idx[:, None] == jnp.arange(num_cols)[None, :]).astype(jnp.float32) * live_mask[
        :, None
    ]
    total = jnp.einsum("tc,tix->cix", placing, products, precision=lax.Precision.HIGHEST)
    return total.reshape(num_cols * tile_size, width)


def body(features, adj_tiles, tile_rows, tile_cols, tile_count, weight, cotangent):
    width = features.shape[1]
    own_nodes = features.shape[0]
    row_count = lax.axis_size("row")
    col_count = lax.axis_size("col")
    my_tiles = adj_tiles[0]
    my_cols = tile_cols[0]
    count = tile_count[0, 0]
    position = lax.axis_index("col")
    offsets = (tile_rows[0] - position) % col_count
    w_self = weight[:width]
    w_neigh = weight[width:]
    col_feats = lax.all_gather(features, "row", axis=0, tiled=True)
    projected = jnp.dot(col_feats, w_neigh, preferred_element_type=jnp.float32).astype(jnp.bfloat16)
    stacked_sums = tile_forward(my_tiles, offsets, my_cols, count, projected, REACH)
    neighbour = stacked_sums[0]
    for step in range(1, REACH):
        neighbour = neighbour + from_behind(stacked_sums[step], "col", step)
    pre_act = jnp.dot(features, w_self, preferred_element_type=jnp.float32) + neighbour
    hidden = jax.nn.silu(pre_act).astype(jnp.bfloat16)
    sigmoid_z = jax.nn.sigmoid(pre_act)
    slope = sigmoid_z * (1.0 + pre_act * (1.0 - sigmoid_z))
    upstream = (cotangent.astype(jnp.float32) * slope).astype(jnp.bfloat16)
    grad_self = jnp.dot(features.T, upstream, preferred_element_type=jnp.float32)
    window_rows = [upstream]
    for step in range(1, REACH):
        window_rows.append(from_behind(upstream, "col", -step))
    window = jnp.concatenate(window_rows, axis=0)
    spread = tile_backward(my_tiles, offsets, my_cols, count, window, row_count)
    grad_neigh = jnp.dot(col_feats.astype(jnp.float32).T, spread, precision=lax.Precision.HIGHEST)
    stacked = jnp.concatenate([grad_self, grad_neigh], axis=0)
    summed = lax.psum(stacked, ("row", "col"))
    total_nodes = own_nodes * row_count * col_count
    weight_grad = summed * float(total_nodes) ** (-0.5)
    return (hidden, weight_grad)


def solution(mesh):
    in_specs = (
        P(("row", "col"), None),
        P("row", "col", None, None),
        P("row", "col"),
        P("row", "col"),
        P("row", "col"),
        P(),
        P(("row", "col"), None),
    )
    out_specs = (P(("row", "col"), None), P())
    return jax.shard_map(body, mesh=mesh, in_specs=in_specs, out_specs=out_specs, check_vma=False)
```

profile of v0, /device:TPU:0, one launch (start us, length us, event | category | flops | bytes accessed | tf_op | source)
XLA Modules:
  0.0 212.7 jit_solution(5097959716192634621)
XLA Ops:
  7.2 0.0 all-reduce.2.cloned.1.call-start
  7.2 0.7 compare_select_fusion.1
  7.9 0.7 compare_and_fusion.1
  8.6 11.8 %all_gather.3 = bf16[512,512]{1,0:T(8,128)(2,1)S(1)} all-gather(bf16[128,512]{1,0:T(8,128)(2,1)} %param.9), channel_id=1, replica_groups=mesh['row'=4,'col'=8] {'row'}, dimensions={0}, use_global_device_ids=true | all-gather | bytes 655360 | tf_op jit(solution)/shard_map/all_gather | solution.py:54
  20.4 1.7 convolution_convert_fusion
  22.1 0.6 gather_fusion
  22.7 1.9 fusion.6
  24.6 2.3 %copy.18 = f32[8,512,128]{1,0,2:T(8,128)S(1)} copy(f32[8,512,128]{2,1,0:T(8,128)} %fusion.6) | data formatting | bytes 4194304 | tf_op jit(solution)/shard_map/tij,tjx->tix/dot_general | solution.py:20
  27.6 1.8 fusion.2
  29.4 0.8 fusion.37
  30.2 0.1 collective-permute-start.2
  30.3 1.6 collective-permute-start.1
  32.0 2.5 %collective-permute-start = (f32[128,512]{1,0:T(8,128)S(1)}, f32[128,512]{1,0:T(8,128)S(1)}, u32[]{:S(2)}, u32[]{:S(2)}) collective-permute-start(f32[128,512]{1,0:T(8,128)S(1)} %bitcast.64), channel_id=1, source_target_pairs={{0,1},{1,2},{2,3},{3,4},{4,5},{5,6},{6,7},{7,0},{8,9},{9,10},{10,1... | collective-permute-start | bytes 786440 | tf_op jit(solution)/shard_map/ppermute | solution.py:12
  34.4 16.6 %collective-permute-done.2 = f32[128,512]{1,0:T(8,128)S(1)} collective-permute-done((f32[128,512]{1,0:T(8,128)S(1)}, f32[128,512]{1,0:T(8,128)S(1)}, u32[]{:S(2)}, u32[]{:S(2)}) %collective-permute-start.2) | collective-permute-done | bytes 262176 | tf_op jit(solution)/shard_map/ppermute | solution.py:12
  51.1 1.0 multiply_convert_fusion
  52.1 0.8 collective-permute-start.4
  52.9 1.1 collective-permute-start.3
  54.0 1.3 convolution_bitcast_fusion
  55.3 3.3 %collective-permute-done.5 = bf16[128,512]{1,0:T(8,128)(2,1)S(1)} collective-permute-done((bf16[128,512]{1,0:T(8,128)(2,1)S(1)}, bf16[128,512]{1,0:T(8,128)(2,1)S(1)}, u32[]{:S(2)}, u32[]{:S(2)}) %collective-permute-start.5) | collective-permute-done | bytes 131104 | tf_op jit(solution)/shard_map/ppermute | solution.py:12
  58.6 0.8 collective-permute-done.4
  59.4 0.6 gather_fusion.1
  60.1 0.6 fusion.4
  60.6 2.0 copy.19
  62.6 3.4 %fusion = f32[4,128,512]{2,0,1:T(4,128)S(1)} fusion(f32[8,512,128]{1,0,2:T(8,128)} %copy.19, s32[8]{0:T(128)S(1)} %bitcast.65, f32[8]{0:T(128)S(1)} %get-tuple-element.11), kind=kOutput, calls=%fused_computation.3 | convolution fusion | flops 25165888 | bytes 3145792 | tf_op jit(solution)/shard_map/tc,tix->cix/dot_general | solution.py:38
  66.1 0.3 copy.17
  66.4 1.1 convolution_bitcast_fusion.1
  67.5 1.5 pad_maximum_fusion
  69.0 0.0 all-reduce.2.cloned.1.call-update
  69.0 0.9 copy-done.5
  70.0 0.7 multiply_convert_fusion.1
  70.7 132.1 %all-reduce.2.cloned.1.call-done = f32[1024,512]{1,0:T(8,128)} async-done(((f32[1024,512]{1,0:T(8,128)}), f32[1024,512]{1,0:T(8,128)}) %all-reduce.2.cloned.1.call-update) | async-done | bytes 2097168 | tf_op jit(solution)/shard_map/psum | solution.py:73
  202.8 3.1 %broadcast_multiply_fusion = f32[1024,512]{1,0:T(8,128)} fusion(f32[1024,512]{1,0:T(8,128)} %all-reduce.2.cloned.1.call-done), kind=kLoop, calls=%fused_computation.14 | loop fusion | flops 524288 | bytes 4194304 | tf_op jit(solution)/shard_map/mul | solution.py:75
  (31 shorter events, 0.2 us)
Async XLA Ops:
  7.2 15.6 %copy-start = (bf16[1,8,128,128]{3,2,1,0:T(8,128)(2,1)S(1)}, bf16[1,8,128,128]{3,2,1,0:T(8,128)(2,1)}, u32[]{:S(2)}) copy-start(bf16[1,8,128,128]{3,2,1,0:T(8,128)(2,1)} %param.10) | copy-start | bytes 786436
  7.2 195.6 %all-reduce.2.cloned.1.call-start = ((), (), s32[]{:S(2)}) async-start(), calls=%async_computation | async-start | bytes 4194304 | tf_op jit(solution)/shard_map/psum | solution.py:73
  20.4 1.7 copy-start.2
  24.6 2.9 %copy-start.7 = (s32[1,8]{1,0:T(1,128)S(1)}, s32[1,8]{1,0:T(1,128)}, u32[]{:S(2)}) copy-start(s32[1,8]{1,0:T(1,128)} %param.11) | copy-start | bytes 100
  29.4 21.6 %copy-start.4 = (bf16[128,512]{1,0:T(8,128)(2,1)S(1)}, bf16[128,512]{1,0:T(8,128)(2,1)}, u32[]{:S(2)}) copy-start(bf16[128,512]{1,0:T(8,128)(2,1)} %param.9) | copy-start | bytes 393220
  29.4 21.6 %copy-start.8 = (bf16[1024,512]{1,0:T(8,128)(2,1)S(1)}, bf16[1024,512]{1,0:T(8,128)(2,1)}, u32[]{:S(2)}) copy-start(bf16[1024,512]{1,0:T(8,128)(2,1)} %param.14) | copy-start | bytes 3145732
  29.4 21.6 %copy-start.9 = (bf16[128,512]{1,0:T(8,128)(2,1)S(1)}, bf16[128,512]{1,0:T(8,128)(2,1)}, u32[]{:S(2)}) copy-start(bf16[128,512]{1,0:T(8,128)(2,1)} %param.15) | copy-start | bytes 393220
  30.2 20.8 %collective-permute-start.2 = (f32[128,512]{1,0:T(8,128)S(1)}, f32[128,512]{1,0:T(8,128)S(1)}, u32[]{:S(2)}, u32[]{:S(2)}) collective-permute-start(f32[128,512]{1,0:T(8,128)S(1)} %bitcast.62), channel_id=1, source_target_pairs={{0,3},{1,4},{2,5},{3,6},{4,7},{5,0},{6,1},{7,2},{8,11},{9,12},{10,... | collective-permute-start | bytes 786440 | tf_op jit(solution)/shard_map/ppermute | solution.py:12
  30.3 20.7 %collective-permute-start.1 = (f32[128,512]{1,0:T(8,128)S(1)}, f32[128,512]{1,0:T(8,128)S(1)}, u32[]{:S(2)}, u32[]{:S(2)}) collective-permute-start(f32[128,512]{1,0:T(8,128)S(1)} %bitcast.63), channel_id=1, source_target_pairs={{0,2},{1,3},{2,4},{3,5},{4,6},{5,7},{6,0},{7,1},{8,10},{9,11},{10,... | collective-permute-start | bytes 786440 | tf_op jit(solution)/shard_map/ppermute | solution.py:12
  32.0 19.1 %collective-permute-start = (f32[128,512]{1,0:T(8,128)S(1)}, f32[128,512]{1,0:T(8,128)S(1)}, u32[]{:S(2)}, u32[]{:S(2)}) collective-permute-start(f32[128,512]{1,0:T(8,128)S(1)} %bitcast.64), channel_id=1, source_target_pairs={{0,1},{1,2},{2,3},{3,4},{4,5},{5,6},{6,7},{7,0},{8,9},{9,10},{10,1... | collective-permute-start | bytes 786440 | tf_op jit(solution)/shard_map/ppermute | solution.py:12
  52.1 6.6 %collective-permute-start.5 = (bf16[128,512]{1,0:T(8,128)(2,1)S(1)}, bf16[128,512]{1,0:T(8,128)(2,1)S(1)}, u32[]{:S(2)}, u32[]{:S(2)}) collective-permute-start(bf16[128,512]{1,0:T(8,128)(2,1)S(1)} %get-tuple-element.5), channel_id=1, source_target_pairs={{0,5},{1,6},{2,7},{3,0},{4,1},{5,2},{6,3},{7,4},{8,13},{9,14},{10,... | collective-permute-start | bytes 393224 | tf_op jit(solution)/shard_map/ppermute | solution.py:12
  52.1 7.3 %collective-permute-start.4 = (bf16[128,512]{1,0:T(8,128)(2,1)S(1)}, bf16[128,512]{1,0:T(8,128)(2,1)S(1)}, u32[]{:S(2)}, u32[]{:S(2)}) collective-permute-start(bf16[128,512]{1,0:T(8,128)(2,1)S(1)} %get-tuple-element.5), channel_id=1, source_target_pairs={{0,6},{1,7},{2,0},{3,1},{4,2},{5,3},{6,4},{7,5},{8,14},{9,15},{10,... | collective-permute-start | bytes 393224 | tf_op jit(solution)/shard_map/ppermute | solution.py:12
  52.9 6.5 %collective-permute-start.3 = (bf16[128,512]{1,0:T(8,128)(2,1)S(1)}, bf16[128,512]{1,0:T(8,128)(2,1)S(1)}, u32[]{:S(2)}, u32[]{:S(2)}) collective-permute-start(bf16[128,512]{1,0:T(8,128)(2,1)S(1)} %get-tuple-element.5), channel_id=1, source_target_pairs={{0,7},{1,0},{2,1},{3,2},{4,3},{5,4},{6,5},{7,6},{8,15},{9,8},{10,9... | collective-permute-start | bytes 393224 | tf_op jit(solution)/shard_map/ppermute | solution.py:12
  60.6 2.0 copy-start.6
  62.6 3.8 %copy-start.3 = (bf16[512,512]{1,0:T(8,128)(2,1)S(1)}, bf16[512,512]{1,0:T(8,128)(2,1)}, u32[]{:S(2)}) copy-start(bf16[512,512]{1,0:T(8,128)(2,1)} %copy-done.2) | copy-start | bytes 1572868
  66.1 1.5 copy-start.1
  69.0 0.9 copy-start.5
Sparse Core Ops, SparseCore 0:
  69.2 133.5 all-reduce.1
where the time goes:
time: 213 us
  waiting for transfers between devices  153 us (72%)
  between operations  14.9 us (7%)
  matrix products  12.8 us (6%)
  blocking collectives  11.8 us (6%)
  local copies, waits for them, and re-layouts  7.59 us (4%)
  other arithmetic  6.79 us (3%)
  starting transfers between devices  6.07 us (3%)
    psum x1, waiting for transfers between devices, body(): summed = lax.psum(stacked, ('row', 'col'))  132 us
    ppermute x6, waiting for transfers between devices, from_behind(): return lax.ppermute(value, axis, pairs)  20.7 us
    all_gather x1, blocking collectives, body(): col_feats = lax.all_gather(features, 'row', axis=0, tiled=True)  11.8 us
    ppermute x6, starting transfers between devices, from_behind(): return lax.ppermute(value, axis, pairs)  6.03 us
  transfers between devices with their start and end apart: 7, of which 4 were waited for; matrix products, arithmetic and copies ran while one was open for 1% of the time, Pallas kernels for 0%

commit v1 on v0

v1 whole, which is shorter than its diff:
```python
import jax
import jax.numpy as jnp
from jax import lax
from jax.sharding import PartitionSpec as P

REACH = 4


def from_behind(value, axis, steps):
    count = lax.axis_size(axis)
    pairs = [(source, (source + steps) % count) for source in range(count)]
    return lax.ppermute(value, axis, pairs)


def split(value):
    high = value.astype(jnp.bfloat16)
    return high, (value - high.astype(jnp.float32)).astype(jnp.bfloat16)


def dot(a, b):
    return jnp.dot(a, b, preferred_element_type=jnp.float32)


def body(features, adj_tiles, tile_rows, tile_cols, tile_count, weight, cotangent):
    width = features.shape[1]
    own_nodes = features.shape[0]
    row_count = lax.axis_size("row")
    col_count = lax.axis_size("col")
    tiles = adj_tiles[0]
    slots, size = tiles.shape[:2]
    position = lax.axis_index("col")
    offsets = (tile_rows[0] - position) % col_count
    live = jnp.arange(slots) < tile_count[0, 0]
    col_feats = lax.all_gather(features, "row", axis=0, tiled=True)
    chosen = jnp.take(col_feats.reshape(-1, size, width), tile_cols[0], axis=0).reshape(slots * size, width)
    placed = (offsets[None, :] == jnp.arange(REACH)[:, None]) & live[None, :]
    masked = jnp.where(placed[:, None, :, None], tiles.transpose(1, 0, 2)[None], 0)
    sums = dot(masked.reshape(REACH * size, slots * size), chosen).reshape(REACH, size, width)
    total = sums[0]
    for step in range(1, REACH):
        total = total + from_behind(sums[step], "col", step)
    high, low = split(total)
    pre_act = dot(features, weight[:width]) + dot(high, weight[width:]) + dot(low, weight[width:])
    hidden = jax.nn.silu(pre_act).astype(jnp.bfloat16)
    sigmoid_z = jax.nn.sigmoid(pre_act)
    slope = sigmoid_z * (1.0 + pre_act * (1.0 - sigmoid_z))
    upstream = (cotangent.astype(jnp.float32) * slope).astype(jnp.bfloat16)
    grad_self = dot(features.T, upstream)
    grad_neigh = dot(high.T, upstream) + dot(low.T, upstream)
    stacked = jnp.concatenate([grad_self, grad_neigh], axis=0)
    summed = lax.psum(stacked, ("row", "col"))
    total_nodes = own_nodes * row_count * col_count
    return hidden, summed * float(total_nodes) ** (-0.5)


def solution(mesh):
    in_specs = (
        P(("row", "col"), None),
        P("row", "col", None, None),
        P("row", "col"),
        P("row", "col"),
        P("row", "col"),
        P(),
        P(("row", "col"), None),
    )
    out_specs = (P(("row", "col"), None), P())
    return jax.shard_map(body, mesh=mesh, in_specs=in_specs, out_specs=out_specs, check_vma=False)
```

time: 213 us -> 192 us (0.901)
  matrix products: 12.8 us -> 3.13 us
  local copies, waits for them, and re-layouts: 7.59 us -> 1.81 us
  waiting for transfers between devices: 153 us -> 148 us
    dot_general x8 -> x7, matrix products: 12.8 us -> 3.13 us  [dot(): return jnp.dot(a, b, preferred_element_type=jnp.float32)]
    dot_general x3 -> x0, local copies, waits for them, and re-layouts: 4.56 us -> none  [the longest x1 2.26 us: tile_forward(): jnp.einsum('tij,tjx->tix', adj_tiles, chosen, preferred_element_type=jnp....]
    ppermute x6 -> x3, waiting for transfers between devices: 20.7 us -> 17 us  [from_behind(): return lax.ppermute(value, axis, pairs)]
    ppermute x6 -> x3, starting transfers between devices: 6.03 us -> 4.49 us  [from_behind(): return lax.ppermute(value, axis, pairs)]
  transfers between devices with their start and end apart: 7 -> 4, of which waited for: 4 -> 3; matrix products, arithmetic and copies ran while one was open for 1% -> 0% of each run, Pallas kernels for 0% -> 0%
where the time goes in v1:
time: 192 us; the launch traced here: 191 us
  waiting for transfers between devices  148 us (77%)
  between operations  14.8 us (8%)
  blocking collectives  11.8 us (6%)
  other arithmetic  7.04 us (4%)
  starting transfers between devices  4.53 us (2%)
  matrix products  3.13 us (2%)
    psum x1, waiting for transfers between devices, body(): summed = lax.psum(stacked, ('row', 'col'))  131 us
    ppermute x3, waiting for transfers between devices, from_behind(): return lax.ppermute(value, axis, pairs)  17 us
    all_gather x1, blocking collectives, body(): col_feats = lax.all_gather(features, 'row', axis=0, tiled=True)  11.8 us
    ppermute x3, starting transfers between devices, from_behind(): return lax.ppermute(value, axis, pairs)  4.49 us
  transfers between devices with their start and end apart: 4, of which 3 were waited for; matrix products, arithmetic and copies ran while one was open for 0% of the time, Pallas kernels for 0%

profile of v1, /device:TPU:0, one launch (start us, length us, event | category | flops | bytes accessed | tf_op | source)
XLA Modules:
  0.0 191.3 jit_solution(7985509843229283211)
XLA Ops:
  7.2 0.0 all-reduce.2.cloned.1.call-start
  7.2 0.7 fusion.12
  7.9 0.7 compare_and_fusion
  9.2 1.1 copy.9
  10.3 11.8 %all_gather.3 = bf16[512,512]{1,0:T(8,128)(2,1)S(1)} all-gather(bf16[128,512]{1,0:T(8,128)(2,1)} %param.7), channel_id=1, replica_groups=mesh['row'=4,'col'=8] {'row'}, dimensions={0}, use_global_device_ids=true | all-gather | bytes 655360 | tf_op jit(solution)/shard_map/all_gather | solution.py:34
  22.2 0.7 fusion.10
  22.9 0.6 gather_fusion
  23.5 0.2 broadcast_select_fusion
  23.7 0.1 broadcast_select_fusion.1
  23.8 0.0 copy-start
  23.8 0.0 copy-start.1
  23.8 0.7 fusion
  24.5 0.1 fusion.16
  24.6 0.0 copy-start.2
  24.6 0.1 collective-permute-start
  24.7 2.9 %collective-permute-start.2 = (f32[128,512]{1,0:T(8,128)S(1)}, f32[128,512]{1,0:T(8,128)S(1)}, u32[]{:S(2)}, u32[]{:S(2)}) collective-permute-start(f32[128,512]{1,0:T(8,128)S(1)} %get-tuple-element.3), channel_id=1, source_target_pairs={{0,3},{1,4},{2,5},{3,6},{4,7},{5,0},{6,1},{7,2},{8,11},{9,12},{10,... | collective-permute-start | bytes 786440 | tf_op jit(solution)/shard_map/ppermute | solution.py:12
  27.5 1.6 collective-permute-start.1
  29.1 0.0 copy-done
  29.1 0.2 fusion.3
  29.3 3.9 %collective-permute-done = f32[128,512]{1,0:T(8,128)S(1)} collective-permute-done((f32[128,512]{1,0:T(8,128)S(1)}, f32[128,512]{1,0:T(8,128)S(1)}, u32[]{:S(2)}, u32[]{:S(2)}) %collective-permute-start) | collective-permute-done | bytes 262176 | tf_op jit(solution)/shard_map/ppermute | solution.py:12
  33.2 13.1 %collective-permute-done.2 = f32[128,512]{1,0:T(8,128)S(1)} collective-permute-done((f32[128,512]{1,0:T(8,128)S(1)}, f32[128,512]{1,0:T(8,128)S(1)}, u32[]{:S(2)}, u32[]{:S(2)}) %collective-permute-start.2) | collective-permute-done | bytes 262176 | tf_op jit(solution)/shard_map/ppermute | solution.py:12
  46.3 0.0 collective-permute-done.1
  46.3 0.1 fusion.8
  46.4 0.2 convolution_add_fusion.2
  46.6 1.0 multiply_convert_fusion
  47.6 0.3 fusion.15
  48.0 0.3 convolution_bitcast_fusion
  48.3 0.3 convolution_add_fusion
  48.6 1.5 pad_maximum_fusion
  50.1 0.0 all-reduce.2.cloned.1.call-update
  50.1 131.2 %all-reduce.2.cloned.1.call-done = f32[1024,512]{1,0:T(8,128)} async-done(((f32[1024,512]{1,0:T(8,128)}), f32[1024,512]{1,0:T(8,128)}) %all-reduce.2.cloned.1.call-update) | async-done | bytes 2097168 | tf_op jit(solution)/shard_map/psum | solution.py:51
  181.3 3.1 %broadcast_multiply_fusion = f32[1024,512]{1,0:T(8,128)} fusion(f32[1024,512]{1,0:T(8,128)} %all-reduce.2.cloned.1.call-done), kind=kLoop, calls=%fused_computation.9 | loop fusion | flops 524288 | bytes 4194304 | tf_op jit(solution)/shard_map/mul | solution.py:53
  (5 shorter events, 0.0 us)
Async XLA Ops:
  7.2 174.2 %all-reduce.2.cloned.1.call-start = ((), (), s32[]{:S(2)}) async-start(), calls=%async_computation | async-start | bytes 4194304 | tf_op jit(solution)/shard_map/psum | solution.py:51
  23.8 5.3 %copy-start = (bf16[128,512]{1,0:T(8,128)(2,1)S(1)}, bf16[128,512]{1,0:T(8,128)(2,1)}, u32[]{:S(2)}) copy-start(bf16[128,512]{1,0:T(8,128)(2,1)} %param.7) | copy-start | bytes 393220
  23.8 5.3 %copy-start.1 = (bf16[1024,512]{1,0:T(8,128)(2,1)S(1)}, bf16[1024,512]{1,0:T(8,128)(2,1)}, u32[]{:S(2)}) copy-start(bf16[1024,512]{1,0:T(8,128)(2,1)} %param.12) | copy-start | bytes 3145732
  24.6 22.0 %copy-start.2 = (bf16[128,512]{1,0:T(8,128)(2,1)S(1)}, bf16[128,512]{1,0:T(8,128)(2,1)}, u32[]{:S(2)}) copy-start(bf16[128,512]{1,0:T(8,128)(2,1)} %param.13) | copy-start | bytes 393220
  24.6 8.6 %collective-permute-start = (f32[128,512]{1,0:T(8,128)S(1)}, f32[128,512]{1,0:T(8,128)S(1)}, u32[]{:S(2)}, u32[]{:S(2)}) collective-permute-start(f32[128,512]{1,0:T(8,128)S(1)} %get-tuple-element.2), channel_id=1, source_target_pairs={{0,1},{1,2},{2,3},{3,4},{4,5},{5,6},{6,7},{7,0},{8,9},{9,10},{10,1... | collective-permute-start | bytes 786440 | tf_op jit(solution)/shard_map/ppermute | solution.py:12
  24.7 21.6 %collective-permute-start.2 = (f32[128,512]{1,0:T(8,128)S(1)}, f32[128,512]{1,0:T(8,128)S(1)}, u32[]{:S(2)}, u32[]{:S(2)}) collective-permute-start(f32[128,512]{1,0:T(8,128)S(1)} %get-tuple-element.3), channel_id=1, source_target_pairs={{0,3},{1,4},{2,5},{3,6},{4,7},{5,0},{6,1},{7,2},{8,11},{9,12},{10,... | collective-permute-start | bytes 786440 | tf_op jit(solution)/shard_map/ppermute | solution.py:12
  27.5 18.8 %collective-permute-start.1 = (f32[128,512]{1,0:T(8,128)S(1)}, f32[128,512]{1,0:T(8,128)S(1)}, u32[]{:S(2)}, u32[]{:S(2)}) collective-permute-start(f32[128,512]{1,0:T(8,128)S(1)} %get-tuple-element.4), channel_id=1, source_target_pairs={{0,2},{1,3},{2,4},{3,5},{4,6},{5,7},{6,0},{7,1},{8,10},{9,11},{10,... | collective-permute-start | bytes 786440 | tf_op jit(solution)/shard_map/ppermute | solution.py:12
Sparse Core Ops, SparseCore 0:
  50.3 131.0 all-reduce.1

commit v2 on v1

--- a/solution.py
+++ b/solution.py
@@ -1,6 +1,10 @@
+import functools
+
 import jax
 import jax.numpy as jnp
 from jax import lax
+from jax.experimental import pallas as pl
+from jax.experimental.pallas import tpu as pltpu
 from jax.sharding import PartitionSpec as P
 
 REACH = 4
@@ -19,6 +23,206 @@
 
 def dot(a, b):
     return jnp.dot(a, b, preferred_element_type=jnp.float32)
+
+
+MESH = pl.DeviceIdType.MESH
+
+
+def kernel(n_row, n_col, scale, features, tiles, rows, cols, count, weight, cotangent, hidden, grad,
+           slab, chosen, part, arrived, left_high, left_low, give, taken, up_give, up_taken,
+           term, term_in, piece, piece_in, own_part, self_part, send, recv):
+    r, c = lax.axis_index("row"), lax.axis_index("col")
+    core, z = lax.rem(c, 2), lax.div(c, 2)
+    n_z = n_col // 2
+    size, width = features.shape
+    slots = tiles.shape[0]
+    sibling = (r, c + 1 - 2 * core)
+    counter = iter(range(1000))
+
+    def copy(source, target, landing, device):
+        slot = next(counter)
+        out = pltpu.make_async_remote_copy(source, target, send.at[slot], recv.at[slot], device, MESH)
+        into = pltpu.make_async_remote_copy(landing, landing, send.at[slot], recv.at[slot], device, MESH)
+        return out, into
+
+    barrier = pltpu.get_barrier_semaphore()
+    row_peers = [(lax.rem(r + d, n_row), c) for d in range(1, n_row)]
+    col_peers = [(r, lax.rem(c + d, n_col)) for d in range(1, n_col)]
+    for peer in row_peers + col_peers:
+        pl.semaphore_signal(barrier, inc=1, device_id=peer, device_id_type=MESH)
+    pl.semaphore_wait(barrier, len(row_peers) + len(col_peers))
+
+    sent = []
+
+    def start(out):
+        out.start()
+        sent.append(out)
+
+    gathers = []
+    for d in range(1, n_row):
+        out, into = copy(features, slab.at[r], slab.at[lax.rem(r + n_row - d, n_row)], (lax.rem(r + d, n_row), c))
+        start(out)
+        gathers.append(into)
+    slab[r] = features[...]
+    self_part[...] = dot(features[...], weight[:width])
+    for into in gathers:
+        into.wait_recv()
+
+    for s in range(slots):
+        chosen[s * size:(s + 1) * size, :] = slab[cols[0, s]]
+    live = count[0, 0]
+    offsets = [lax.rem(rows[0, s] - c + n_col, n_col) for s in range(slots)]
+
+    def block_sum(k):
+        masked = [
+            jnp.where(jnp.logical_and(offsets[s] == k, s < live), tiles[s], jnp.zeros_like(tiles[s]))
+            for s in range(slots)
+        ]
+        return dot(jnp.concatenate(masked, axis=1), chosen[...])
+
+    incoming = []
+    for k in range(REACH - 1, 0, -1):
+        part[k - 1] = block_sum(k).astype(jnp.bfloat16)
+        out, into = copy(part.at[k - 1], arrived.at[k - 1], arrived.at[k - 1], (r, lax.rem(c + k, n_col)))
+        start(out)
+        incoming.append(into)
+    own_part[...] = block_sum(0)
+    total = own_part[...]
+    for k, into in zip(range(REACH - 1, 0, -1), incoming):
+        into.wait_recv()
+        total = total + arrived[k - 1].astype(jnp.float32)
+
+    high, low = split(total)
+    first = core == 0
+    empty = jnp.zeros_like(high)
+    give[0] = jnp.where(first, high, features[...])
+    give[1] = jnp.where(first, low, empty)
+    out, lefts = copy(give, taken, taken, sibling)
+    start(out)
+    left_high[:, :size] = jnp.where(first, features[...], high).T
+    left_low[:, :size] = jnp.where(first, empty, low).T
+
+    pre_act = self_part[...] + dot(high, weight[width:]) + dot(low, weight[width:])
+    gate = 1.0 / (1.0 + jnp.exp(-pre_act))
+    hidden[...] = (pre_act * gate).astype(jnp.bfloat16)
+    slope = gate * (1.0 + pre_act * (1.0 - gate))
+    up_give[...] = (cotangent[...].astype(jnp.float32) * slope).astype(jnp.bfloat16)
+    out, ups = copy(up_give, up_taken, up_taken, sibling)
+    start(out)
+    lefts.wait_recv()
+    left_high[:, size:] = taken[0].T
+    left_low[:, size:] = taken[1].T
+    ups.wait_recv()
+    upstream = jnp.concatenate([up_give[...], up_taken[...]], axis=0)
+
+    share = width // n_row
+    small = share // n_z
+
+    def rows_of(q):
+        at = pl.ds(pl.multiple_of(q * share, share), share)
+        return dot(left_high[at, :], upstream) + dot(left_low[at, :], upstream)
+
+    incoming = []
+    for d in range(1, n_row):
+        q = lax.rem(r + d, n_row)
+        term[d - 1] = rows_of(q).astype(jnp.bfloat16)
+        out, into = copy(term.at[d - 1], term_in.at[d - 1], term_in.at[d - 1], (q, c))
+        start(out)
+        incoming.append(into)
+    total = rows_of(r)
+    for d, into in enumerate(incoming):
+        into.wait_recv()
+        total = total + term_in[d].astype(jnp.float32)
+    piece[...] = total
+    incoming = []
+    for d in range(1, n_z):
+        q = lax.rem(z + d, n_z)
+        at = pl.ds(pl.multiple_of(q * small, small), small)
+        out, into = copy(piece.at[at], piece_in.at[d - 1], piece_in.at[d - 1], (r, 2 * q + core))
+        start(out)
+        incoming.append(into)
+    total = piece[pl.ds(pl.multiple_of(z * small, small), small), :]
+    for d, into in enumerate(incoming):
+        into.wait_recv()
+        total = total + piece_in[d]
+
+    def region(half, q, level):
+        return grad.at[pl.ds(pl.multiple_of(half * width + q * share + level * small, small), small)]
+
+    def band(half, q):
+        return grad.at[pl.ds(pl.multiple_of(half * width + q * share, share), share)]
+
+    mine = region(core, r, z)
+    mine[...] = (total * scale).astype(jnp.bfloat16)
+    incoming = []
+    for d in range(1, n_z):
+        q = lax.rem(z + d, n_z)
+        out, into = copy(mine, mine, region(core, r, lax.rem(z + n_z - d, n_z)), (r, 2 * q + core))
+        start(out)
+        incoming.append(into)
+    for into in incoming:
+        into.wait_recv()
+    incoming = []
+    mine = band(core, r)
+    for d in range(1, n_row):
+        out, into = copy(mine, mine, band(core, lax.rem(r + n_row - d, n_row)), (lax.rem(r + d, n_row), c))
+        start(out)
+        incoming.append(into)
+    last = []
+    for d in range(n_row):
+        q = lax.rem(r + n_row - d, n_row)
+        if d > 0:
+            incoming[d - 1].wait_recv()
+        out, into = copy(band(core, q), band(core, q), band(1 - core, q), sibling)
+        start(out)
+        last.append(into)
+    for into in last:
+        into.wait_recv()
+    for out in sent:
+        out.wait_send()
+
+
+def fused(features, tiles, rows, cols, count, weight, cotangent, n_row, n_col):
+    size, width = features.shape
+    slots = tiles.shape[0]
+    share = width // n_row
+    small = share // (n_col // 2)
+    half, full = jnp.bfloat16, jnp.float32
+    copies = 3 * (n_row - 1) + (REACH - 1) + 2 * (n_col // 2 - 1) + 2 + n_row
+    vmem = pl.BlockSpec(memory_space=pltpu.VMEM)
+    smem = pl.BlockSpec(memory_space=pltpu.SMEM)
+    return pl.pallas_call(
+        functools.partial(kernel, n_row, n_col, float(size * n_row * n_col) ** (-0.5)),
+        out_shape=(
+            jax.ShapeDtypeStruct((size, width), half),
+            jax.ShapeDtypeStruct((2 * width, width), half),
+        ),
+        in_specs=[vmem, vmem, smem, smem, smem, vmem, vmem],
+        out_specs=(vmem, vmem),
+        scratch_shapes=[
+            pltpu.VMEM((n_row, size, width), half),
+            pltpu.VMEM((slots * size, width), half),
+            pltpu.VMEM((REACH - 1, size, width), half),
+            pltpu.VMEM((REACH - 1, size, width), half),
+            pltpu.VMEM((width, 2 * size), half),
+            pltpu.VMEM((width, 2 * size), half),
+            pltpu.VMEM((2, size, width), half),
+            pltpu.VMEM((2, size, width), half),
+            pltpu.VMEM((size, width), half),
+            pltpu.VMEM((size, width), half),
+            pltpu.VMEM((n_row - 1, share, width), half),
+            pltpu.VMEM((n_row - 1, share, width), half),
+            pltpu.VMEM((share, width), full),
+            pltpu.VMEM((n_col // 2 - 1, small, width), full),
+            pltpu.VMEM((size, width), full),
+            pltpu.VMEM((size, width), full),
+            pltpu.SemaphoreType.DMA((copies,)),
+            pltpu.SemaphoreType.DMA((copies,)),
+        ],
+        compiler_params=pltpu.CompilerParams(
+            collective_id=0, has_side_effects=True, vmem_limit_bytes=40 * 1024 * 1024
+        ),
+    )(features, tiles, rows, cols, count, weight, cotangent)
 
 
 def body(features, adj_tiles, tile_rows, tile_cols, tile_count, weight, cotangent):
@@ -28,6 +232,13 @@
     col_count = lax.axis_size("col")
     tiles = adj_tiles[0]
     slots, size = tiles.shape[:2]
+    share = width // row_count
+    small = share // (col_count // 2)
+    if col_count % 2 == 0 and REACH <= col_count and small >= 16 and small % 16 == 0:
+        hidden, grad = fused(
+            features, tiles, tile_rows, tile_cols, tile_count, weight, cotangent, row_count, col_count
+        )
+        return hidden, grad.astype(jnp.float32)
     position = lax.axis_index("col")
     offsets = (tile_rows[0] - position) % col_count
     live = jnp.arange(slots) < tile_count[0, 0]

time: 192 us -> 61.3 us (0.32)
  waiting for transfers between devices: 148 us -> 0 us
  Pallas kernels: 0 us -> 52.2 us
  between operations: 14.8 us -> 1.3 us
  blocking collectives: 11.8 us -> 0 us
  other arithmetic: 7.04 us -> 1.61 us
  starting transfers between devices: 4.53 us -> 0 us
  local copies, waits for them, and re-layouts: 1.81 us -> 5.94 us
  matrix products: 3.13 us -> 0 us
    psum x1 -> x0, waiting for transfers between devices: 131 us -> none  [body(): summed = lax.psum(stacked, ('row', 'col'))]
    pallas_call x0 -> x1, Pallas kernels: none -> 52.2 us  [fused(): pl.pallas_call(functools.partial(kernel, n_row, n_col, float(size * n_row...]
    ppermute x3 -> x0, waiting for transfers between devices: 17 us -> none  [from_behind(): return lax.ppermute(value, axis, pairs)]
    all_gather x1 -> x0, blocking collectives: 11.8 us -> none  [body(): col_feats = lax.all_gather(features, 'row', axis=0, tiled=True)]
    unnamed x6 -> x13, local copies, waits for them, and re-layouts: 0.02 us -> 5.94 us
    ppermute x3 -> x0, starting transfers between devices: 4.49 us -> none  [from_behind(): return lax.ppermute(value, axis, pairs)]
    mul x1 -> x0, other arithmetic: 3.14 us -> none  [body(): return (hidden, summed * float(total_nodes) ** (-0.5))]
    dot_general x7 -> x0, matrix products: 3.13 us -> none  [dot(): return jnp.dot(a, b, preferred_element_type=jnp.float32)]
  transfers between devices with their start and end apart: 4 -> 0, of which waited for: 3 -> 0; matrix products, arithmetic and copies ran while one was open for 0% -> 0% of each run, Pallas kernels for 0% -> 0%
where the time goes in v2:
time: 61.3 us; the launch traced here: 61 us
  Pallas kernels  52.2 us (85%)
  local copies, waits for them, and re-layouts  5.94 us (10%)
  other arithmetic  1.61 us (3%)
  between operations  1.3 us (2%)
    pallas_call x1, Pallas kernels, fused(): pl.pallas_call(functools.partial(kernel, n_row, n_col, float(size * n_row...  52.2 us
    unnamed x13, local copies, waits for them, and re-layouts  5.94 us
    convert_element_type x1, other arithmetic, body(): return (hidden, grad.astype(jnp.float32))  1.61 us

profile of v2, /device:TPU:0, one launch (start us, length us, event | category | flops | bytes accessed | tf_op | source)
XLA Modules:
  0.0 61.0 jit_solution(17366315899525290637)
XLA Ops:
  1.3 0.0 copy-start
  1.3 1.2 %copy-done = bf16[1024,512]{1,0:T(8,128)(2,1)S(1)} copy-done((bf16[1024,512]{1,0:T(8,128)(2,1)S(1)}, bf16[1024,512]{1,0:T(8,128)(2,1)}, u32[]{:S(2)}) %copy-start) | copy-done | bytes 1048600
  2.5 0.0 copy-start.1
  2.5 0.9 %copy-done.1 = bf16[1,8,128,128]{3,2,1,0:T(8,128)(2,1)S(1)} copy-done((bf16[1,8,128,128]{3,2,1,0:T(8,128)(2,1)S(1)}, bf16[1,8,128,128]{3,2,1,0:T(8,128)(2,1)}, u32[]{:S(2)}) %copy-start.1) | copy-done | bytes 262168
  3.5 0.0 copy-start.2
  3.5 0.9 %copy-done.2 = bf16[128,512]{1,0:T(8,128)(2,1)S(1)} copy-done((bf16[128,512]{1,0:T(8,128)(2,1)S(1)}, bf16[128,512]{1,0:T(8,128)(2,1)}, u32[]{:S(2)}) %copy-start.2) | copy-done | bytes 131096
  4.4 0.0 copy-start.3
  4.4 0.9 %copy-done.3 = bf16[128,512]{1,0:T(8,128)(2,1)S(1)} copy-done((bf16[128,512]{1,0:T(8,128)(2,1)S(1)}, bf16[128,512]{1,0:T(8,128)(2,1)}, u32[]{:S(2)}) %copy-start.3) | copy-done | bytes 131096
  5.3 0.0 copy-start.4
  5.3 0.7 %copy-done.4 = s32[1,8]{1,0:T(1,128)S(1)} copy-done((s32[1,8]{1,0:T(1,128)S(1)}, s32[1,8]{1,0:T(1,128)}, u32[]{:S(2)}) %copy-start.4) | copy-done | bytes 56
  5.9 0.0 copy-start.5
  5.9 0.7 %copy-done.5 = s32[1,8]{1,0:T(1,128)S(1)} copy-done((s32[1,8]{1,0:T(1,128)S(1)}, s32[1,8]{1,0:T(1,128)}, u32[]{:S(2)}) %copy-start.5) | copy-done | bytes 56
  6.6 52.2 %shard_map.86 = (bf16[128,512]{1,0:T(8,128)(2,1)S(1)}, bf16[1024,512]{1,0:T(8,128)(2,1)S(1)}) custom-call(bf16[128,512]{1,0:T(8,128)(2,1)S(1)} %copy-done.2, bf16[8,128,128]{2,1,0:T(8,128)(2,1)S(1)} %bitcast.1, s32[1,8]{1,0:T(1,128)S(1)} %copy-done.4, s32[1,8]{1,0:T(1,128)S(1)} %copy-done.5, s32[1,1]{1,0:T(1,128)S(6)} %copy.10.count, ...), custom_call_target="tpu_custom_call" | custom-call | tf_op jit(solution)/shard_map/pallas_call | solution.py:194
  58.7 1.6 %convert_element_type.3 = f32[1024,512]{1,0:T(8,128)} convert(bf16[1024,512]{1,0:T(8,128)(2,1)S(1)} %get-tuple-element.5) | non-fusion elementwise | flops 524288 | bytes 3145728 | tf_op jit(solution)/shard_map/convert_element_type | solution.py:241
  60.4 0.7 %copy.11 = bf16[128,512]{1,0:T(8,128)(2,1)} copy(bf16[128,512]{1,0:T(8,128)(2,1)S(1)} %get-tuple-element.8) | data formatting | bytes 262144
Async XLA Ops:
  1.3 1.2 %copy-start = (bf16[1024,512]{1,0:T(8,128)(2,1)S(1)}, bf16[1024,512]{1,0:T(8,128)(2,1)}, u32[]{:S(2)}) copy-start(bf16[1024,512]{1,0:T(8,128)(2,1)} %weight.1) | copy-start | bytes 3145732
  2.5 0.9 %copy-start.1 = (bf16[1,8,128,128]{3,2,1,0:T(8,128)(2,1)S(1)}, bf16[1,8,128,128]{3,2,1,0:T(8,128)(2,1)}, u32[]{:S(2)}) copy-start(bf16[1,8,128,128]{3,2,1,0:T(8,128)(2,1)} %param.8) | copy-start | bytes 786436
  3.5 0.9 %copy-start.2 = (bf16[128,512]{1,0:T(8,128)(2,1)S(1)}, bf16[128,512]{1,0:T(8,128)(2,1)}, u32[]{:S(2)}) copy-start(bf16[128,512]{1,0:T(8,128)(2,1)} %features.1) | copy-start | bytes 393220
  4.4 0.9 %copy-start.3 = (bf16[128,512]{1,0:T(8,128)(2,1)S(1)}, bf16[128,512]{1,0:T(8,128)(2,1)}, u32[]{:S(2)}) copy-start(bf16[128,512]{1,0:T(8,128)(2,1)} %cotangent.1) | copy-start | bytes 393220
  5.3 0.7 %copy-start.4 = (s32[1,8]{1,0:T(1,128)S(1)}, s32[1,8]{1,0:T(1,128)}, u32[]{:S(2)}) copy-start(s32[1,8]{1,0:T(1,128)} %rows.1) | copy-start | bytes 100
  5.9 0.7 %copy-start.5 = (s32[1,8]{1,0:T(1,128)S(1)}, s32[1,8]{1,0:T(1,128)}, u32[]{:S(2)}) copy-start(s32[1,8]{1,0:T(1,128)} %cols.1) | copy-start | bytes 100

commit v3 on v1

--- a/solution.py
+++ b/solution.py
@@ -1,6 +1,10 @@
+import functools
+
 import jax
 import jax.numpy as jnp
 from jax import lax
+from jax.experimental import pallas as pl
+from jax.experimental.pallas import tpu as pltpu
 from jax.sharding import PartitionSpec as P
 
 REACH = 4
@@ -19,6 +23,273 @@
 
 def dot(a, b):
     return jnp.dot(a, b, preferred_element_type=jnp.float32)
+
+
+MESH = pl.DeviceIdType.MESH
+PARTS = 2
+
+
+def kernel(n_row, n_col, scale, features, tiles_in, rows, cols, count, weight_in, cotangent_in, hidden_out, grad_out,
+           tiles, weight, cotangent, hidden, grad, masked, chosen, part, arrived, left_high, left_low,
+           give, taken, up_give, up_taken, term, term_in, piece, piece_in, own_part, self_part, send, recv, local, *slabs):
+    r, c = lax.axis_index("row"), lax.axis_index("col")
+    core, z = lax.rem(c, 2), lax.div(c, 2)
+    n_z = n_col // 2
+    size, width = features.shape
+    slots = tiles.shape[0]
+    wide = width // PARTS
+    sibling = (r, c + 1 - 2 * core)
+    counter = iter(range(1000))
+    local_counter = iter(range(1000))
+
+    def copy(source, target, landing, device):
+        slot = next(counter)
+        out = pltpu.make_async_remote_copy(source, target, send.at[slot], recv.at[slot], device, MESH)
+        into = pltpu.make_async_remote_copy(landing, landing, send.at[slot], recv.at[slot], device, MESH)
+        return out, into
+
+    def bring(source, target):
+        moved = pltpu.make_async_copy(source, target, local.at[next(local_counter)])
+        moved.start()
+        return moved
+
+    def columns(p):
+        return pl.ds(p * wide, wide)
+
+    barrier = pltpu.get_barrier_semaphore()
+    row_peers = [(lax.rem(r + d, n_row), c) for d in range(1, n_row)]
+    col_peers = [(r, lax.rem(c + d, n_col)) for d in range(1, n_col)]
+    for peer in row_peers + col_peers:
+        pl.semaphore_signal(barrier, inc=1, device_id=peer, device_id_type=MESH)
+    own_feats = [bring(features.at[:, columns(p)], slabs[p].at[r]) for p in range(PARTS)]
+    tiles_here = bring(tiles_in, tiles)
+    weight_here = bring(weight_in, weight)
+    cotangent_here = bring(cotangent_in, cotangent)
+    pl.semaphore_wait(barrier, len(row_peers) + len(col_peers))
+
+    sent = []
+
+    def start(out):
+        out.start()
+        sent.append(out)
+
+    gathers = []
+    for p in range(PARTS):
+        gathers.append([])
+        for d in range(1, n_row):
+            out, into = copy(features.at[:, columns(p)], slabs[p].at[r],
+                             slabs[p].at[lax.rem(r + n_row - d, n_row)], (lax.rem(r + d, n_row), c))
+            start(out)
+            gathers[p].append(into)
+
+    live = count[0, 0]
+    offsets = [lax.rem(rows[0, s] - c + n_col, n_col) for s in range(slots)]
+    tiles_here.wait()
+    for k in range(REACH):
+        for s in range(slots):
+            masked[k, :, s * size:(s + 1) * size] = jnp.where(
+                jnp.logical_and(offsets[s] == k, s < live), tiles[s], jnp.zeros_like(tiles[s])
+            )
+    for moved in own_feats:
+        moved.wait()
+    weight_here.wait()
+    feats = jnp.concatenate([slabs[p][r] for p in range(PARTS)], axis=1)
+    self_part[...] = dot(feats, weight[:width])
+    cotangent_here.wait()
+
+    sums = []
+    for p in range(PARTS):
+        for into in gathers[p]:
+            into.wait_recv()
+        for s in range(slots):
+            chosen[p, s * size:(s + 1) * size, :] = slabs[p][cols[0, s]]
+        sums.append([])
+        for k in range(REACH - 1, 0, -1):
+            part[p, k - 1] = dot(masked[k], chosen[p]).astype(jnp.bfloat16)
+            out, into = copy(part.at[p, k - 1], arrived.at[p, k - 1], arrived.at[p, k - 1], (r, lax.rem(c + k, n_col)))
+            start(out)
+            sums[p].append((k, into))
+        own_part[p] = dot(masked[0], chosen[p])
+
+    first = core == 0
+    lefts = []
+    highs, lows = [], []
+    for p in range(PARTS):
+        total = own_part[p]
+        for k, into in sums[p]:
+            into.wait_recv()
+            total = total + arrived[p, k - 1].astype(jnp.float32)
+        high, low = split(total)
+        highs.append(high)
+        lows.append(low)
+        mine = slabs[p][r]
+        empty = jnp.zeros_like(high)
+        give[p, 0] = jnp.where(first, high, mine)
+        give[p, 1] = jnp.where(first, low, empty)
+        out, into = copy(give.at[p], taken.at[p], taken.at[p], sibling)
+        start(out)
+        lefts.append(into)
+        left_high[p * wide:(p + 1) * wide, :size] = jnp.where(first, mine, high).T
+        left_low[p * wide:(p + 1) * wide, :size] = jnp.where(first, empty, low).T
+
+    high = jnp.concatenate(highs, axis=1)
+    low = jnp.concatenate(lows, axis=1)
+    ups = []
+    for p in range(PARTS):
+        at = slice(p * wide, (p + 1) * wide)
+        pre_act = self_part[:, at] + dot(high, weight[width:, at]) + dot(low, weight[width:, at])
+        gate = 1.0 / (1.0 + jnp.exp(-pre_act))
+        slope = gate * (1.0 + pre_act * (1.0 - gate))
+        up_give[p] = (cotangent[:, at].astype(jnp.float32) * slope).astype(jnp.bfloat16)
+        out, into = copy(up_give.at[p], up_taken.at[p], up_taken.at[p], sibling)
+        start(out)
+        ups.append(into)
+        hidden[:, at] = (pre_act * gate).astype(jnp.bfloat16)
+    placed = [bring(hidden, hidden_out)]
+    for p in range(PARTS):
+        lefts[p].wait_recv()
+        left_high[p * wide:(p + 1) * wide, size:] = taken[p, 0].T
+        left_low[p * wide:(p + 1) * wide, size:] = taken[p, 1].T
+
+    share = width // n_row
+    small = share // n_z
+
+    def block(half, q, level, p):
+        return grad.at[pl.ds(pl.multiple_of(half * width + q * share + level * small, small), small), columns(p)]
+
+    def band(half, q, p):
+        return grad.at[pl.ds(pl.multiple_of(half * width + q * share, share), share), columns(p)]
+
+    waiting = []
+    for p in range(PARTS):
+        ups[p].wait_recv()
+        upstream = jnp.concatenate([up_give[p], up_taken[p]], axis=0)
+        waiting.append([])
+        for d in range(n_row - 1, -1, -1):
+            q = lax.rem(r + d, n_row)
+            at = pl.ds(pl.multiple_of(q * share, share), share)
+            value = dot(left_high[at, :], upstream) + dot(left_low[at, :], upstream)
+            if d == 0:
+                piece[p] = value
+                continue
+            term[p, d - 1] = value.astype(jnp.bfloat16)
+            out, into = copy(term.at[p, d - 1], term_in.at[p, d - 1], term_in.at[p, d - 1], (q, c))
+            start(out)
+            waiting[p].append((d, into))
+    over_z = []
+    for p in range(PARTS):
+        total = piece[p]
+        for d, into in waiting[p]:
+            into.wait_recv()
+            total = total + term_in[p, d - 1].astype(jnp.float32)
+        piece[p] = total
+        over_z.append([])
+        for d in range(1, n_z):
+            q = lax.rem(z + d, n_z)
+            at = pl.ds(pl.multiple_of(q * small, small), small)
+            out, into = copy(piece.at[p, at], piece_in.at[p, d - 1], piece_in.at[p, d - 1], (r, 2 * q + core))
+            start(out)
+            over_z[p].append((d, into))
+
+    back_z = []
+    for p in range(PARTS):
+        total = piece[p, pl.ds(pl.multiple_of(z * small, small), small), :]
+        for d, into in over_z[p]:
+            into.wait_recv()
+            total = total + piece_in[p, d - 1]
+        mine = block(core, r, z, p)
+        mine[...] = (total * scale).astype(jnp.bfloat16)
+        back_z.append([])
+        for d in range(1, n_z):
+            out, into = copy(mine, mine, block(core, r, lax.rem(z + n_z - d, n_z), p),
+                             (r, 2 * lax.rem(z + d, n_z) + core))
+            start(out)
+            back_z[p].append(into)
+    back_row = []
+    last = []
+
+    def pass_on(q, p):
+        out, into = copy(band(core, q, p), band(core, q, p), band(1 - core, q, p), sibling)
+        start(out)
+        last.append((into, q, p))
+
+    for p in range(PARTS):
+        for into in back_z[p]:
+            into.wait_recv()
+        mine = band(core, r, p)
+        back_row.append([])
+        for d in range(1, n_row):
+            q = lax.rem(r + n_row - d, n_row)
+            out, into = copy(mine, mine, band(core, q, p), (lax.rem(r + d, n_row), c))
+            start(out)
+            back_row[p].append((q, into))
+        pass_on(r, p)
+    for p in range(PARTS):
+        for q, into in back_row[p]:
+            into.wait_recv()
+            pass_on(q, p)
+    half = pl.ds(pl.multiple_of(core * width, width), width)
+    placed.append(bring(grad.at[half], grad_out.at[half]))
+    for into, q, p in last:
+        into.wait_recv()
+    half = pl.ds(pl.multiple_of((1 - core) * width, width), width)
+    placed.append(bring(grad.at[half], grad_out.at[half]))
+    for moved in placed:
+        moved.wait()
+    for out in sent:
+        out.wait_send()
+
+
+def fused(features, tiles, rows, cols, count, weight, cotangent, n_row, n_col):
+    size, width = features.shape
+    slots = tiles.shape[0]
+    wide = width // PARTS
+    share = width // n_row
+    n_z = n_col // 2
+    small = share // n_z
+    half, full = jnp.bfloat16, jnp.float32
+    copies = PARTS * (3 * (n_row - 1) + (REACH - 1) + 2 * (n_z - 1) + 2 + n_row)
+    hbm = pl.BlockSpec(memory_space=pl.ANY)
+    smem = pl.BlockSpec(memory_space=pltpu.SMEM)
+    return pl.pallas_call(
+        functools.partial(kernel, n_row, n_col, float(size * n_row * n_col) ** (-0.5)),
+        out_shape=(
+            jax.ShapeDtypeStruct((size, width), half),
+            jax.ShapeDtypeStruct((2 * width, width), half),
+        ),
+        in_specs=[hbm, hbm, smem, smem, smem, hbm, hbm],
+        out_specs=(hbm, hbm),
+        scratch_shapes=[
+            pltpu.VMEM(tiles.shape, half),
+            pltpu.VMEM(weight.shape, half),
+            pltpu.VMEM((size, width), half),
+            pltpu.VMEM((size, width), half),
+            pltpu.VMEM((2 * width, width), half),
+            pltpu.VMEM((REACH, size, slots * size), half),
+            pltpu.VMEM((PARTS, slots * size, wide), half),
+            pltpu.VMEM((PARTS, REACH - 1, size, wide), half),
+            pltpu.VMEM((PARTS, REACH - 1, size, wide), half),
+            pltpu.VMEM((width, 2 * size), half),
+            pltpu.VMEM((width, 2 * size), half),
+            pltpu.VMEM((PARTS, 2, size, wide), half),
+            pltpu.VMEM((PARTS, 2, size, wide), half),
+            pltpu.VMEM((PARTS, size, wide), half),
+            pltpu.VMEM((PARTS, size, wide), half),
+            pltpu.VMEM((PARTS, n_row - 1, share, wide), half),
+            pltpu.VMEM((PARTS, n_row - 1, share, wide), half),
+            pltpu.VMEM((PARTS, share, wide), full),
+            pltpu.VMEM((PARTS, n_z - 1, small, wide), full),
+            pltpu.VMEM((PARTS, size, wide), full),
+            pltpu.VMEM((size, width), full),
+            pltpu.SemaphoreType.DMA((copies,)),
+            pltpu.SemaphoreType.DMA((copies,)),
+            pltpu.SemaphoreType.DMA((PARTS + 6,)),
+            *[pltpu.VMEM((n_row, size, wide), half)] * PARTS,
+        ],
+        compiler_params=pltpu.CompilerParams(
+            collective_id=0, has_side_effects=True, vmem_limit_bytes=60 * 1024 * 1024
+        ),
+    )(features, tiles, rows, cols, count, weight, cotangent)
 
 
 def body(features, adj_tiles, tile_rows, tile_cols, tile_count, weight, cotangent):
@@ -28,6 +299,13 @@
     col_count = lax.axis_size("col")
     tiles = adj_tiles[0]
     slots, size = tiles.shape[:2]
+    share = width // row_count
+    small = share // (col_count // 2)
+    if col_count % 2 == 0 and REACH <= col_count and small >= 16 and small % 16 == 0:
+        hidden, grad = fused(
+            features, tiles, tile_rows, tile_cols, tile_count, weight, cotangent, row_count, col_count
+        )
+        return hidden, grad.astype(jnp.float32)
     position = lax.axis_index("col")
     offsets = (tile_rows[0] - position) % col_count
     live = jnp.arange(slots) < tile_count[0, 0]

time: 192 us -> 51.8 us (0.27)
  waiting for transfers between devices: 148 us -> 0 us
  Pallas kernels: 0 us -> 46 us
  between operations: 14.8 us -> 1.29 us
  blocking collectives: 11.8 us -> 0 us
  starting transfers between devices: 4.53 us -> 0 us
  other arithmetic: 7.04 us -> 2.87 us
  matrix products: 3.13 us -> 0 us
    psum x1 -> x0, waiting for transfers between devices: 131 us -> none  [body(): summed = lax.psum(stacked, ('row', 'col'))]
    pallas_call x0 -> x1, Pallas kernels: none -> 46 us  [fused(): pl.pallas_call(functools.partial(kernel, n_row, n_col, float(size * n_row...]
    ppermute x3 -> x0, waiting for transfers between devices: 17 us -> none  [from_behind(): return lax.ppermute(value, axis, pairs)]
    all_gather x1 -> x0, blocking collectives: 11.8 us -> none  [body(): col_feats = lax.all_gather(features, 'row', axis=0, tiled=True)]
    ppermute x3 -> x0, starting transfers between devices: 4.49 us -> none  [from_behind(): return lax.ppermute(value, axis, pairs)]
    mul x1 -> x0, other arithmetic: 3.14 us -> none  [body(): return (hidden, summed * float(total_nodes) ** (-0.5))]
    dot_general x7 -> x0, matrix products: 3.13 us -> none  [dot(): return jnp.dot(a, b, preferred_element_type=jnp.float32)]
    convert_element_type x0 -> x1, other arithmetic: none -> 2.87 us  [body(): return (hidden, grad.astype(jnp.float32))]
  transfers between devices with their start and end apart: 4 -> 0, of which waited for: 3 -> 0; matrix products, arithmetic and copies ran while one was open for 0% -> 0% of each run, Pallas kernels for 0% -> 0%
where the time goes in v3:
time: 51.8 us; the launch traced here: 50.8 us
  Pallas kernels  46 us (89%)
  other arithmetic  2.87 us (6%)
  between operations  1.29 us (2%)
  local copies, waits for them, and re-layouts  0.66 us (1%)
    pallas_call x1, Pallas kernels, fused(): pl.pallas_call(functools.partial(kernel, n_row, n_col, float(size * n_row...  46 us
    convert_element_type x1, other arithmetic, body(): return (hidden, grad.astype(jnp.float32))  2.87 us

profile of v3, /device:TPU:0, one launch (start us, length us, event | category | flops | bytes accessed | tf_op | source)
XLA Modules:
  0.0 50.8 jit_solution(8585378037580873154)
XLA Ops:
  1.3 46.0 %shard_map.86 = (bf16[128,512]{1,0:T(8,128)(2,1)}, bf16[1024,512]{1,0:T(8,128)(2,1)}) custom-call(bf16[128,512]{1,0:T(8,128)(2,1)} %features.1, bf16[8,128,128]{2,1,0:T(8,128)(2,1)} %bitcast.1, s32[1,8]{1,0:T(1,128)} %rows.1, s32[1,8]{1,0:T(1,128)} %cols.1, s32[1,1]{1,0:T(1,128)S(6)} %copy.10.count, bf16[1024,512]{1,0:T(8,128)(2,1)} %weight_in.1, ...), custom_call_target="tpu_custom_call" | custom-call | tf_op jit(solution)/shard_map/pallas_call | solution.py:254
  47.3 0.0 copy-start
  47.3 2.9 %convert_element_type.3 = f32[1024,512]{1,0:T(8,128)} convert(bf16[1024,512]{1,0:T(8,128)(2,1)} %get-tuple-element.5) | non-fusion elementwise | flops 524288 | bytes 3145728 | tf_op jit(solution)/shard_map/convert_element_type | solution.py:308
  50.2 0.0 copy-done
  50.2 0.7 %copy.11 = bf16[128,512]{1,0:T(8,128)(2,1)} copy(bf16[128,512]{1,0:T(8,128)(2,1)S(1)} %copy-done) | data formatting | bytes 262144
Async XLA Ops:
  47.3 2.9 %copy-start = (bf16[128,512]{1,0:T(8,128)(2,1)S(1)}, bf16[128,512]{1,0:T(8,128)(2,1)}, u32[]{:S(2)}) copy-start(bf16[128,512]{1,0:T(8,128)(2,1)} %get-tuple-element.8) | copy-start | bytes 393220

commit v4 on v3

--- a/solution.py
+++ b/solution.py
@@ -29,9 +29,16 @@
 PARTS = 2
 
 
-def kernel(n_row, n_col, scale, features, tiles_in, rows, cols, count, weight_in, cotangent_in, hidden_out, grad_out,
-           tiles, weight, cotangent, hidden, grad, masked, chosen, part, arrived, left_high, left_low,
-           give, taken, up_give, up_taken, term, term_in, piece, piece_in, own_part, self_part, send, recv, local, *slabs):
+def flip(index, bits):
+    for bit in (1, 2, 4, 8, 16):
+        if bits & bit:
+            index = index + bit - 2 * bit * lax.rem(lax.div(index, bit), 2)
+    return index
+
+
+def kernel(n_row, n_col, scale, features, tiles_in, rows, cols, count, weight_in, cotangent_in, hidden, grad_out,
+           tiles, weight, cotangent, grad, wide_grad, masked, chosen, part, arrived, swap, swap_in, left_high, left_low,
+           give, taken, up_give, up_taken, term, term_in, piece, near_in, far, far_in, own_part, self_part, send, recv, local, *slabs):
     r, c = lax.axis_index("row"), lax.axis_index("col")
     core, z = lax.rem(c, 2), lax.div(c, 2)
     n_z = n_col // 2
@@ -103,22 +110,29 @@
             into.wait_recv()
         for s in range(slots):
             chosen[p, s * size:(s + 1) * size, :] = slabs[p][cols[0, s]]
-        sums.append([])
-        for k in range(REACH - 1, 0, -1):
-            part[p, k - 1] = dot(masked[k], chosen[p]).astype(jnp.bfloat16)
-            out, into = copy(part.at[p, k - 1], arrived.at[p, k - 1], arrived.at[p, k - 1], (r, lax.rem(c + k, n_col)))
-            start(out)
-            sums[p].append((k, into))
+        part[p, 0] = dot(masked[1 + 2 * core], chosen[p]).astype(jnp.bfloat16)
+        out, straight = copy(part.at[p, 0], arrived.at[p, 0], arrived.at[p, 0],
+                             (r, lax.rem(c + 1 + 2 * core, n_col)))
+        start(out)
+        swap[p] = dot(masked[3 - 2 * core], chosen[p])
+        out, into = copy(swap.at[p], swap_in.at[p], swap_in.at[p], sibling)
+        start(out)
+        joined = dot(masked[2], chosen[p])
         own_part[p] = dot(masked[0], chosen[p])
+        into.wait_recv()
+        part[p, 1] = (joined + swap_in[p]).astype(jnp.bfloat16)
+        out, into = copy(part.at[p, 1], arrived.at[p, 1], arrived.at[p, 1], (r, lax.rem(c + 2, n_col)))
+        start(out)
+        sums.append([straight, into])
 
     first = core == 0
     lefts = []
     highs, lows = [], []
     for p in range(PARTS):
         total = own_part[p]
-        for k, into in sums[p]:
-            into.wait_recv()
-            total = total + arrived[p, k - 1].astype(jnp.float32)
+        for k, into in enumerate(sums[p]):
+            into.wait_recv()
+            total = total + arrived[p, k].astype(jnp.float32)
         high, low = split(total)
         highs.append(high)
         lows.append(low)
@@ -145,7 +159,6 @@
         start(out)
         ups.append(into)
         hidden[:, at] = (pre_act * gate).astype(jnp.bfloat16)
-    placed = [bring(hidden, hidden_out)]
     for p in range(PARTS):
         lefts[p].wait_recv()
         left_high[p * wide:(p + 1) * wide, size:] = taken[p, 0].T
@@ -184,10 +197,14 @@
             total = total + term_in[p, d - 1].astype(jnp.float32)
         piece[p] = total
         over_z.append([])
-        for d in range(1, n_z):
-            q = lax.rem(z + d, n_z)
+        for d in range(n_z - 1, 0, -1):
+            q = flip(z, d)
             at = pl.ds(pl.multiple_of(q * small, small), small)
-            out, into = copy(piece.at[p, at], piece_in.at[p, d - 1], piece_in.at[p, d - 1], (r, 2 * q + core))
+            if d == 1:
+                out, into = copy(piece.at[p, at], near_in.at[p], near_in.at[p], (r, 2 * q + core))
+            else:
+                far[p, d - 2] = piece[p, at, :].astype(jnp.bfloat16)
+                out, into = copy(far.at[p, d - 2], far_in.at[p, d - 2], far_in.at[p, d - 2], (r, 2 * q + core))
             start(out)
             over_z[p].append((d, into))
 
@@ -196,7 +213,7 @@
         total = piece[p, pl.ds(pl.multiple_of(z * small, small), small), :]
         for d, into in over_z[p]:
             into.wait_recv()
-            total = total + piece_in[p, d - 1]
+            total = total + (near_in[p] if d == 1 else far_in[p, d - 2].astype(jnp.float32))
         mine = block(core, r, z, p)
         mine[...] = (total * scale).astype(jnp.bfloat16)
         back_z.append([])
@@ -208,10 +225,18 @@
     back_row = []
     last = []
 
+    placed = []
+
+    def deliver(half, q, p):
+        at = (pl.ds(pl.multiple_of(half * width + q * share, share), share), columns(p))
+        wide_grad[at] = grad[at].astype(jnp.float32)
+        placed.append(bring(wide_grad.at[at], grad_out.at[at]))
+
     def pass_on(q, p):
         out, into = copy(band(core, q, p), band(core, q, p), band(1 - core, q, p), sibling)
         start(out)
         last.append((into, q, p))
+        deliver(core, q, p)
 
     for p in range(PARTS):
         for into in back_z[p]:
@@ -228,12 +253,9 @@
         for q, into in back_row[p]:
             into.wait_recv()
             pass_on(q, p)
-    half = pl.ds(pl.multiple_of(core * width, width), width)
-    placed.append(bring(grad.at[half], grad_out.at[half]))
     for into, q, p in last:
         into.wait_recv()
-    half = pl.ds(pl.multiple_of((1 - core) * width, width), width)
-    placed.append(bring(grad.at[half], grad_out.at[half]))
+        deliver(1 - core, q, p)
     for moved in placed:
         moved.wait()
     for out in sent:
@@ -250,25 +272,28 @@
     half, full = jnp.bfloat16, jnp.float32
     copies = PARTS * (3 * (n_row - 1) + (REACH - 1) + 2 * (n_z - 1) + 2 + n_row)
     hbm = pl.BlockSpec(memory_space=pl.ANY)
+    vmem = pl.BlockSpec(memory_space=pltpu.VMEM)
     smem = pl.BlockSpec(memory_space=pltpu.SMEM)
     return pl.pallas_call(
         functools.partial(kernel, n_row, n_col, float(size * n_row * n_col) ** (-0.5)),
         out_shape=(
             jax.ShapeDtypeStruct((size, width), half),
-            jax.ShapeDtypeStruct((2 * width, width), half),
+            jax.ShapeDtypeStruct((2 * width, width), full),
         ),
         in_specs=[hbm, hbm, smem, smem, smem, hbm, hbm],
-        out_specs=(hbm, hbm),
+        out_specs=(vmem, hbm),
         scratch_shapes=[
             pltpu.VMEM(tiles.shape, half),
             pltpu.VMEM(weight.shape, half),
             pltpu.VMEM((size, width), half),
-            pltpu.VMEM((size, width), half),
             pltpu.VMEM((2 * width, width), half),
+            pltpu.VMEM((2 * width, width), full),
             pltpu.VMEM((REACH, size, slots * size), half),
             pltpu.VMEM((PARTS, slots * size, wide), half),
-            pltpu.VMEM((PARTS, REACH - 1, size, wide), half),
-            pltpu.VMEM((PARTS, REACH - 1, size, wide), half),
+            pltpu.VMEM((PARTS, 2, size, wide), half),
+            pltpu.VMEM((PARTS, 2, size, wide), half),
+            pltpu.VMEM((PARTS, size, wide), full),
+            pltpu.VMEM((PARTS, size, wide), full),
             pltpu.VMEM((width, 2 * size), half),
             pltpu.VMEM((width, 2 * size), half),
             pltpu.VMEM((PARTS, 2, size, wide), half),
@@ -278,12 +303,14 @@
             pltpu.VMEM((PARTS, n_row - 1, share, wide), half),
             pltpu.VMEM((PARTS, n_row - 1, share, wide), half),
             pltpu.VMEM((PARTS, share, wide), full),
-            pltpu.VMEM((PARTS, n_z - 1, small, wide), full),
+            pltpu.VMEM((PARTS, small, wide), full),
+            pltpu.VMEM((PARTS, n_z - 2, small, wide), half),
+            pltpu.VMEM((PARTS, n_z - 2, small, wide), half),
             pltpu.VMEM((PARTS, size, wide), full),
             pltpu.VMEM((size, width), full),
             pltpu.SemaphoreType.DMA((copies,)),
             pltpu.SemaphoreType.DMA((copies,)),
-            pltpu.SemaphoreType.DMA((PARTS + 6,)),
+            pltpu.SemaphoreType.DMA((PARTS + 3 + 2 * PARTS * n_row,)),
             *[pltpu.VMEM((n_row, size, wide), half)] * PARTS,
         ],
         compiler_params=pltpu.CompilerParams(
@@ -300,12 +327,13 @@
     tiles = adj_tiles[0]
     slots, size = tiles.shape[:2]
     share = width // row_count
+    flippable = col_count // 2 in (4, 8, 16, 32)
     small = share // (col_count // 2)
-    if col_count % 2 == 0 and REACH <= col_count and small >= 16 and small % 16 == 0:
+    if REACH == 4 and col_count % 2 == 0 and flippable and small >= 16 and small % 16 == 0:
         hidden, grad = fused(
             features, tiles, tile_rows, tile_cols, tile_count, weight, cotangent, row_count, col_count
         )
-        return hidden, grad.astype(jnp.float32)
+        return hidden, grad
     position = lax.axis_index("col")
     offsets = (tile_rows[0] - position) % col_count
     live = jnp.arange(slots) < tile_count[0, 0]

time: 51.8 us -> 51 us (0.985)
  local copies, waits for them, and re-layouts: 0.66 us -> 4.65 us
  other arithmetic: 2.87 us -> 0 us
  Pallas kernels: 46 us -> 44.5 us
    unnamed x3 -> x2, local copies, waits for them, and re-layouts: 0.66 us -> 4.65 us
    convert_element_type x1 -> x0, other arithmetic: 2.87 us -> none  [body(): return (hidden, grad.astype(jnp.float32))]
    pallas_call x1, Pallas kernels: 46 us -> 44.5 us  [fused(): pl.pallas_call(functools.partial(kernel, n_row, n_col, float(size * n_row...]
where the time goes in v4:
time: 51 us; the launch traced here: 50.4 us
  Pallas kernels  44.5 us (87%)
  local copies, waits for them, and re-layouts  4.65 us (9%)
  between operations  1.29 us (3%)
    pallas_call x1, Pallas kernels, fused(): pl.pallas_call(functools.partial(kernel, n_row, n_col, float(size * n_row...  44.5 us
    unnamed x2, local copies, waits for them, and re-layouts  4.65 us

profile of v4, /device:TPU:0, one launch (start us, length us, event | category | flops | bytes accessed | tf_op | source)
XLA Modules:
  0.0 50.4 jit_solution(17396358747111389902)
XLA Ops:
  1.3 44.5 %shard_map.86 = (bf16[128,512]{1,0:T(8,128)(2,1)}, f32[1024,512]{1,0:T(8,128)}) custom-call(bf16[128,512]{1,0:T(8,128)(2,1)} %features.1, bf16[8,128,128]{2,1,0:T(8,128)(2,1)} %bitcast.1, s32[1,8]{1,0:T(1,128)} %rows.1, s32[1,8]{1,0:T(1,128)} %cols.1, s32[1,1]{1,0:T(1,128)S(6)} %copy.11.count, bf16[1024,512]{1,0:T(8,128)(2,1)} %weight_in.1, ...), custom_call_target="tpu_custom_call" | custom-call | tf_op jit(solution)/shard_map/pallas_call | solution.py:277
  45.8 1.6 %copy.12 = bf16[128,512]{1,0:T(8,128)(2,1)} copy(bf16[128,512]{1,0:T(8,128)(2,1)} %get-tuple-element.4) | data formatting | bytes 262144
  47.3 3.1 %copy.13 = f32[1024,512]{1,0:T(8,128)} copy(f32[1024,512]{1,0:T(8,128)} %get-tuple-element.5) | data formatting | bytes 4194304

commit v5 on v4

--- a/solution.py
+++ b/solution.py
@@ -36,8 +36,8 @@
     return index
 
 
-def kernel(n_row, n_col, scale, features, tiles_in, rows, cols, count, weight_in, cotangent_in, hidden, grad_out,
-           tiles, weight, cotangent, grad, wide_grad, masked, chosen, part, arrived, swap, swap_in, left_high, left_low,
+def kernel(n_row, n_col, scale, features, tiles_in, rows, cols, count, weight_in, cotangent_in, hidden, grad,
+           tiles, weight, cotangent, masked, chosen, part, arrived, swap, swap_in, left_high, left_low,
            give, taken, up_give, up_taken, term, term_in, piece, near_in, far, far_in, own_part, self_part, send, recv, local, *slabs):
     r, c = lax.axis_index("row"), lax.axis_index("col")
     core, z = lax.rem(c, 2), lax.div(c, 2)
@@ -225,18 +225,10 @@
     back_row = []
     last = []
 
-    placed = []
-
-    def deliver(half, q, p):
-        at = (pl.ds(pl.multiple_of(half * width + q * share, share), share), columns(p))
-        wide_grad[at] = grad[at].astype(jnp.float32)
-        placed.append(bring(wide_grad.at[at], grad_out.at[at]))
-
     def pass_on(q, p):
         out, into = copy(band(core, q, p), band(core, q, p), band(1 - core, q, p), sibling)
         start(out)
         last.append((into, q, p))
-        deliver(core, q, p)
 
     for p in range(PARTS):
         for into in back_z[p]:
@@ -255,9 +247,6 @@
             pass_on(q, p)
     for into, q, p in last:
         into.wait_recv()
-        deliver(1 - core, q, p)
-    for moved in placed:
-        moved.wait()
     for out in sent:
         out.wait_send()
 
@@ -277,17 +266,15 @@
     return pl.pallas_call(
         functools.partial(kernel, n_row, n_col, float(size * n_row * n_col) ** (-0.5)),
         out_shape=(
-            jax.ShapeDtypeStruct((size, width), half),
-            jax.ShapeDtypeStruct((2 * width, width), full),
+            pltpu.VMEM((size, width), half),
+            pltpu.VMEM((2 * width, width), half),
         ),
         in_specs=[hbm, hbm, smem, smem, smem, hbm, hbm],
-        out_specs=(vmem, hbm),
+        out_specs=(vmem, vmem),
         scratch_shapes=[
             pltpu.VMEM(tiles.shape, half),
             pltpu.VMEM(weight.shape, half),
             pltpu.VMEM((size, width), half),
-            pltpu.VMEM((2 * width, width), half),
-            pltpu.VMEM((2 * width, width), full),
             pltpu.VMEM((REACH, size, slots * size), half),
             pltpu.VMEM((PARTS, slots * size, wide), half),
             pltpu.VMEM((PARTS, 2, size, wide), half),
@@ -310,7 +297,7 @@
             pltpu.VMEM((size, width), full),
             pltpu.SemaphoreType.DMA((copies,)),
             pltpu.SemaphoreType.DMA((copies,)),
-            pltpu.SemaphoreType.DMA((PARTS + 3 + 2 * PARTS * n_row,)),
+            pltpu.SemaphoreType.DMA((PARTS + 3,)),
             *[pltpu.VMEM((n_row, size, wide), half)] * PARTS,
         ],
         compiler_params=pltpu.CompilerParams(
@@ -333,7 +320,7 @@
         hidden, grad = fused(
             features, tiles, tile_rows, tile_cols, tile_count, weight, cotangent, row_count, col_count
         )
-        return hidden, grad
+        return hidden, grad.astype(jnp.float32)
     position = lax.axis_index("col")
     offsets = (tile_rows[0] - position) % col_count
     live = jnp.arange(slots) < tile_count[0, 0]

time: 51 us -> 47.1 us (0.924)
  local copies, waits for them, and re-layouts: 4.65 us -> 0.66 us
  other arithmetic: 0 us -> 1.61 us
  Pallas kernels: 44.5 us -> 43.4 us
    unnamed x2 -> x1, local copies, waits for them, and re-layouts: 4.65 us -> 0.66 us
    convert_element_type x0 -> x1, other arithmetic: none -> 1.61 us  [body(): return (hidden, grad.astype(jnp.float32))]
    pallas_call x1, Pallas kernels: 44.5 us -> 43.4 us  [fused(): pl.pallas_call(functools.partial(kernel, n_row, n_col, float(size * n_row...]
where the time goes in v5:
time: 47.1 us; the launch traced here: 47 us
  Pallas kernels  43.4 us (92%)
  other arithmetic  1.61 us (3%)
  between operations  1.29 us (3%)
  local copies, waits for them, and re-layouts  0.66 us (1%)
    pallas_call x1, Pallas kernels, fused(): pl.pallas_call(functools.partial(kernel, n_row, n_col, float(size * n_row...  43.4 us
    convert_element_type x1, other arithmetic, body(): return (hidden, grad.astype(jnp.float32))  1.61 us

profile of v5, /device:TPU:0, one launch (start us, length us, event | category | flops | bytes accessed | tf_op | source)
XLA Modules:
  0.0 47.0 jit_solution(18150407102259217845)
XLA Ops:
  1.3 43.4 %shard_map.86 = (bf16[128,512]{1,0:T(8,128)(2,1)S(1)}, bf16[1024,512]{1,0:T(8,128)(2,1)S(1)}) custom-call(bf16[128,512]{1,0:T(8,128)(2,1)} %features.1, bf16[8,128,128]{2,1,0:T(8,128)(2,1)} %bitcast.1, s32[1,8]{1,0:T(1,128)} %rows.1, s32[1,8]{1,0:T(1,128)} %cols.1, s32[1,1]{1,0:T(1,128)S(6)} %copy.11.count, bf16[1024,512]{1,0:T(8,128)(2,1)} %weight_in.1, ...), custom_call_target="tpu_custom_call" | custom-call | tf_op jit(solution)/shard_map/pallas_call | solution.py:266
  44.7 0.7 %copy.10 = bf16[128,512]{1,0:T(8,128)(2,1)} copy(bf16[128,512]{1,0:T(8,128)(2,1)S(1)} %get-tuple-element.6) | data formatting | bytes 262144
  45.3 1.6 %convert_element_type.3 = f32[1024,512]{1,0:T(8,128)} convert(bf16[1024,512]{1,0:T(8,128)(2,1)S(1)} %get-tuple-element.5) | non-fusion elementwise | flops 524288 | bytes 3145728 | tf_op jit(solution)/shard_map/convert_element_type | solution.py:323

commit v6 on v5

--- a/solution.py
+++ b/solution.py
@@ -38,7 +38,7 @@
 
 def kernel(n_row, n_col, scale, features, tiles_in, rows, cols, count, weight_in, cotangent_in, hidden, grad,
            tiles, weight, cotangent, masked, chosen, part, arrived, swap, swap_in, left_high, left_low,
-           give, taken, up_give, up_taken, term, term_in, piece, near_in, far, far_in, own_part, self_part, send, recv, local, *slabs):
+           give, taken, up_give, up_taken, whole, term, term_in, near, near_in, far, far_in, own_part, self_part, send, recv, local, *slabs):
     r, c = lax.axis_index("row"), lax.axis_index("col")
     core, z = lax.rem(c, 2), lax.div(c, 2)
     n_z = n_col // 2
@@ -125,127 +125,126 @@
         start(out)
         sums.append([straight, into])
 
+    share = width // n_row
+    small = share // n_z
     first = core == 0
+
+    def place(target, p, at, value):
+        for j in range(wide // small):
+            q, rest = divmod(p * wide + j * small, share)
+            target[rest // small, q * small:(q + 1) * small, at] = value[j * small:(j + 1) * small]
+
+    def place_own(p, high, low):
+        place(left_high, p, slice(0, size), jnp.where(first, slabs[p][r], high).T)
+        place(left_low, p, slice(0, size), jnp.where(first, jnp.zeros_like(low), low).T)
+
     lefts = []
-    highs, lows = [], []
     for p in range(PARTS):
         total = own_part[p]
         for k, into in enumerate(sums[p]):
             into.wait_recv()
             total = total + arrived[p, k].astype(jnp.float32)
         high, low = split(total)
-        highs.append(high)
-        lows.append(low)
-        mine = slabs[p][r]
-        empty = jnp.zeros_like(high)
-        give[p, 0] = jnp.where(first, high, mine)
-        give[p, 1] = jnp.where(first, low, empty)
+        give[p, 0] = jnp.where(first, high, slabs[p][r])
+        give[p, 1] = jnp.where(first, low, jnp.zeros_like(low))
         out, into = copy(give.at[p], taken.at[p], taken.at[p], sibling)
         start(out)
         lefts.append(into)
-        left_high[p * wide:(p + 1) * wide, :size] = jnp.where(first, mine, high).T
-        left_low[p * wide:(p + 1) * wide, :size] = jnp.where(first, empty, low).T
-
-    high = jnp.concatenate(highs, axis=1)
-    low = jnp.concatenate(lows, axis=1)
+        if p < PARTS - 1:
+            below = weight[width + p * wide:width + (p + 1) * wide]
+            self_part[...] += dot(high, below) + dot(low, below)
+            place_own(p, high, low)
+
     ups = []
     for p in range(PARTS):
         at = slice(p * wide, (p + 1) * wide)
-        pre_act = self_part[:, at] + dot(high, weight[width:, at]) + dot(low, weight[width:, at])
+        below = weight[2 * width - wide:, at]
+        pre_act = self_part[:, at] + dot(high, below) + dot(low, below)
         gate = 1.0 / (1.0 + jnp.exp(-pre_act))
         slope = gate * (1.0 + pre_act * (1.0 - gate))
-        up_give[p] = (cotangent[:, at].astype(jnp.float32) * slope).astype(jnp.bfloat16)
-        out, into = copy(up_give.at[p], up_taken.at[p], up_taken.at[p], sibling)
+        up_give[:, at] = (cotangent[:, at].astype(jnp.float32) * slope).astype(jnp.bfloat16)
+        out, into = copy(up_give.at[:, at], up_taken.at[:, at], up_taken.at[:, at], sibling)
         start(out)
         ups.append(into)
         hidden[:, at] = (pre_act * gate).astype(jnp.bfloat16)
+    place_own(PARTS - 1, high, low)
     for p in range(PARTS):
         lefts[p].wait_recv()
-        left_high[p * wide:(p + 1) * wide, size:] = taken[p, 0].T
-        left_low[p * wide:(p + 1) * wide, size:] = taken[p, 1].T
-
-    share = width // n_row
-    small = share // n_z
-
-    def block(half, q, level, p):
-        return grad.at[pl.ds(pl.multiple_of(half * width + q * share + level * small, small), small), columns(p)]
-
-    def band(half, q, p):
-        return grad.at[pl.ds(pl.multiple_of(half * width + q * share, share), share), columns(p)]
-
-    waiting = []
-    for p in range(PARTS):
-        ups[p].wait_recv()
-        upstream = jnp.concatenate([up_give[p], up_taken[p]], axis=0)
-        waiting.append([])
-        for d in range(n_row - 1, -1, -1):
-            q = lax.rem(r + d, n_row)
-            at = pl.ds(pl.multiple_of(q * share, share), share)
-            value = dot(left_high[at, :], upstream) + dot(left_low[at, :], upstream)
-            if d == 0:
-                piece[p] = value
-                continue
-            term[p, d - 1] = value.astype(jnp.bfloat16)
-            out, into = copy(term.at[p, d - 1], term_in.at[p, d - 1], term_in.at[p, d - 1], (q, c))
+        place(left_high, p, slice(size, 2 * size), taken[p, 0].T)
+        place(left_low, p, slice(size, 2 * size), taken[p, 1].T)
+    for into in ups:
+        into.wait_recv()
+    upstream = jnp.concatenate([up_give[...], up_taken[...]], axis=0)
+
+    over_row = []
+    for i in range(n_z):
+        level = flip(z, n_z - 1 - i)
+        value = dot(left_high[level], upstream) + dot(left_low[level], upstream)
+        whole[i] = value
+        term[i] = value.astype(jnp.bfloat16)
+        over_row.append([])
+        for e in range(1, n_row):
+            q = lax.rem(r + e, n_row)
+            at = pl.ds(pl.multiple_of(q * small, small), small)
+            out, into = copy(term.at[i, at], term_in.at[i, e - 1], term_in.at[i, e - 1], (q, c))
             start(out)
-            waiting[p].append((d, into))
+            over_row[i].append(into)
     over_z = []
-    for p in range(PARTS):
-        total = piece[p]
-        for d, into in waiting[p]:
+    for i in range(n_z):
+        d = n_z - 1 - i
+        device = (r, 2 * flip(z, d) + core)
+        total = whole[i, pl.ds(pl.multiple_of(r * small, small), small), :]
+        for e, into in enumerate(over_row[i]):
             into.wait_recv()
-            total = total + term_in[p, d - 1].astype(jnp.float32)
-        piece[p] = total
-        over_z.append([])
-        for d in range(n_z - 1, 0, -1):
-            q = flip(z, d)
-            at = pl.ds(pl.multiple_of(q * small, small), small)
-            if d == 1:
-                out, into = copy(piece.at[p, at], near_in.at[p], near_in.at[p], (r, 2 * q + core))
-            else:
-                far[p, d - 2] = piece[p, at, :].astype(jnp.bfloat16)
-                out, into = copy(far.at[p, d - 2], far_in.at[p, d - 2], far_in.at[p, d - 2], (r, 2 * q + core))
-            start(out)
-            over_z[p].append((d, into))
-
+            total = total + term_in[i, e].astype(jnp.float32)
+        if d == 0:
+            break
+        if d == 1:
+            near[...] = total
+            out, into = copy(near, near_in, near_in, device)
+        else:
+            far[d - 2] = total.astype(jnp.bfloat16)
+            out, into = copy(far.at[d - 2], far_in.at[d - 2], far_in.at[d - 2], device)
+        start(out)
+        over_z.append((d, into))
+    for d, into in over_z:
+        into.wait_recv()
+        total = total + (near_in[...] if d == 1 else far_in[d - 2].astype(jnp.float32))
+
+    def block(half, q, level):
+        return grad.at[pl.ds(pl.multiple_of(half * width + q * share + level * small, small), small)]
+
+    mine = block(core, r, z)
+    mine[...] = (total * scale).astype(jnp.bfloat16)
     back_z = []
-    for p in range(PARTS):
-        total = piece[p, pl.ds(pl.multiple_of(z * small, small), small), :]
-        for d, into in over_z[p]:
-            into.wait_recv()
-            total = total + (near_in[p] if d == 1 else far_in[p, d - 2].astype(jnp.float32))
-        mine = block(core, r, z, p)
-        mine[...] = (total * scale).astype(jnp.bfloat16)
-        back_z.append([])
-        for d in range(1, n_z):
-            out, into = copy(mine, mine, block(core, r, lax.rem(z + n_z - d, n_z), p),
-                             (r, 2 * lax.rem(z + d, n_z) + core))
-            start(out)
-            back_z[p].append(into)
+    for d in range(n_z - 1, 0, -1):
+        out, into = copy(mine, mine, block(core, r, flip(z, d)), (r, 2 * flip(z, d) + core))
+        start(out)
+        back_z.append(into)
+    back_z.reverse()
     back_row = []
     last = []
 
-    def pass_on(q, p):
-        out, into = copy(band(core, q, p), band(core, q, p), band(1 - core, q, p), sibling)
-        start(out)
-        last.append((into, q, p))
-
-    for p in range(PARTS):
-        for into in back_z[p]:
-            into.wait_recv()
-        mine = band(core, r, p)
-        back_row.append([])
-        for d in range(1, n_row):
-            q = lax.rem(r + n_row - d, n_row)
-            out, into = copy(mine, mine, band(core, q, p), (lax.rem(r + d, n_row), c))
+    def pass_on(q, level):
+        out, into = copy(block(core, q, level), block(core, q, level), block(1 - core, q, level), sibling)
+        start(out)
+        last.append(into)
+
+    for d in range(n_z):
+        level = flip(z, d)
+        if d > 0:
+            back_z[d - 1].wait_recv()
+        for e in range(1, n_row):
+            q = lax.rem(r + n_row - e, n_row)
+            out, into = copy(block(core, r, level), block(core, r, level), block(core, q, level),
+                             (lax.rem(r + e, n_row), c))
             start(out)
-            back_row[p].append((q, into))
-        pass_on(r, p)
-    for p in range(PARTS):
-        for q, into in back_row[p]:
-            into.wait_recv()
-            pass_on(q, p)
-    for into, q, p in last:
+            back_row.append((q, level, into))
+        pass_on(r, level)
+    for q, level, into in back_row:
+        into.wait_recv()
+        pass_on(q, level)
+    for into in last:
         into.wait_recv()
     for out in sent:
         out.wait_send()
@@ -259,7 +258,7 @@
     n_z = n_col // 2
     small = share // n_z
     half, full = jnp.bfloat16, jnp.float32
-    copies = PARTS * (3 * (n_row - 1) + (REACH - 1) + 2 * (n_z - 1) + 2 + n_row)
+    copies = PARTS * (n_row + 4) + 2 * n_z * (n_row - 1) + 2 * (n_z - 1) + n_z * n_row
     hbm = pl.BlockSpec(memory_space=pl.ANY)
     vmem = pl.BlockSpec(memory_space=pltpu.VMEM)
     smem = pl.BlockSpec(memory_space=pltpu.SMEM)
@@ -281,18 +280,19 @@
             pltpu.VMEM((PARTS, 2, size, wide), half),
             pltpu.VMEM((PARTS, size, wide), full),
             pltpu.VMEM((PARTS, size, wide), full),
-            pltpu.VMEM((width, 2 * size), half),
-            pltpu.VMEM((width, 2 * size), half),
+            pltpu.VMEM((n_z, n_row * small, 2 * size), half),
+            pltpu.VMEM((n_z, n_row * small, 2 * size), half),
             pltpu.VMEM((PARTS, 2, size, wide), half),
             pltpu.VMEM((PARTS, 2, size, wide), half),
-            pltpu.VMEM((PARTS, size, wide), half),
-            pltpu.VMEM((PARTS, size, wide), half),
-            pltpu.VMEM((PARTS, n_row - 1, share, wide), half),
-            pltpu.VMEM((PARTS, n_row - 1, share, wide), half),
-            pltpu.VMEM((PARTS, share, wide), full),
-            pltpu.VMEM((PARTS, small, wide), full),
-            pltpu.VMEM((PARTS, n_z - 2, small, wide), half),
-            pltpu.VMEM((PARTS, n_z - 2, small, wide), half),
+            pltpu.VMEM((size, width), half),
+            pltpu.VMEM((size, width), half),
+            pltpu.VMEM((n_z, n_row * small, width), full),
+            pltpu.VMEM((n_z, n_row * small, width), half),
+            pltpu.VMEM((n_z, n_row - 1, small, width), half),
+            pltpu.VMEM((small, width), full),
+            pltpu.VMEM((small, width), full),
+            pltpu.VMEM((n_z - 2, small, width), half),
+            pltpu.VMEM((n_z - 2, small, width), half),
             pltpu.VMEM((PARTS, size, wide), full),
             pltpu.VMEM((size, width), full),
             pltpu.SemaphoreType.DMA((copies,)),

time: 47.1 us -> 46.7 us (level)
  no operation moved by 1% of the time
where the time goes in v6:
time: 46.7 us; the launch traced here: 46.5 us
  Pallas kernels  43 us (92%)
  other arithmetic  1.61 us (3%)
  between operations  1.29 us (3%)
  local copies, waits for them, and re-layouts  0.66 us (1%)
    pallas_call x1, Pallas kernels, fused(): pl.pallas_call(functools.partial(kernel, n_row, n_col, float(size * n_row...  43 us
    convert_element_type x1, other arithmetic, body(): return (hidden, grad.astype(jnp.float32))  1.61 us

profile of v6, /device:TPU:0, one launch (start us, length us, event | category | flops | bytes accessed | tf_op | source)
XLA Modules:
  0.0 46.5 jit_solution(298063696541644832)
XLA Ops:
  1.3 43.0 %shard_map.86 = (bf16[128,512]{1,0:T(8,128)(2,1)S(1)}, bf16[1024,512]{1,0:T(8,128)(2,1)S(1)}) custom-call(bf16[128,512]{1,0:T(8,128)(2,1)} %features.1, bf16[8,128,128]{2,1,0:T(8,128)(2,1)} %bitcast.1, s32[1,8]{1,0:T(1,128)} %rows.1, s32[1,8]{1,0:T(1,128)} %cols.1, s32[1,1]{1,0:T(1,128)S(6)} %copy.11.count, bf16[1024,512]{1,0:T(8,128)(2,1)} %weight_in.1, ...), custom_call_target="tpu_custom_call" | custom-call | tf_op jit(solution)/shard_map/pallas_call | solution.py:265
  44.3 0.7 %copy.10 = bf16[128,512]{1,0:T(8,128)(2,1)} copy(bf16[128,512]{1,0:T(8,128)(2,1)S(1)} %get-tuple-element.6) | data formatting | bytes 262144
  44.9 1.6 %convert_element_type.3 = f32[1024,512]{1,0:T(8,128)} convert(bf16[1024,512]{1,0:T(8,128)(2,1)S(1)} %get-tuple-element.5) | non-fusion elementwise | flops 524288 | bytes 3145728 | tf_op jit(solution)/shard_map/convert_element_type | solution.py:323

commit v7 on v6

--- a/solution.py
+++ b/solution.py
@@ -26,7 +26,7 @@
 
 
 MESH = pl.DeviceIdType.MESH
-PARTS = 2
+PARTS = 4
 
 
 def flip(index, bits):
@@ -138,6 +138,11 @@
         place(left_high, p, slice(0, size), jnp.where(first, slabs[p][r], high).T)
         place(left_low, p, slice(0, size), jnp.where(first, jnp.zeros_like(low), low).T)
 
+    def place_sibling(p):
+        lefts[p].wait_recv()
+        place(left_high, p, slice(size, 2 * size), taken[p, 0].T)
+        place(left_low, p, slice(size, 2 * size), taken[p, 1].T)
+
     lefts = []
     for p in range(PARTS):
         total = own_part[p]
@@ -154,6 +159,8 @@
             below = weight[width + p * wide:width + (p + 1) * wide]
             self_part[...] += dot(high, below) + dot(low, below)
             place_own(p, high, low)
+            if p > 0:
+                place_sibling(p - 1)
 
     ups = []
     for p in range(PARTS):
@@ -168,10 +175,8 @@
         ups.append(into)
         hidden[:, at] = (pre_act * gate).astype(jnp.bfloat16)
     place_own(PARTS - 1, high, low)
-    for p in range(PARTS):
-        lefts[p].wait_recv()
-        place(left_high, p, slice(size, 2 * size), taken[p, 0].T)
-        place(left_low, p, slice(size, 2 * size), taken[p, 1].T)
+    for p in range(PARTS - 2, PARTS):
+        place_sibling(p)
     for into in ups:
         into.wait_recv()
     upstream = jnp.concatenate([up_give[...], up_taken[...]], axis=0)

time: 46.7 us -> 49 us (1.049)
  Pallas kernels: 43 us -> 45.3 us
    pallas_call x1, Pallas kernels: 43 us -> 45.3 us  [fused(): pl.pallas_call(functools.partial(kernel, n_row, n_col, float(size * n_row...]
where the time goes in v7:
time: 49 us; the launch traced here: 48.8 us
  Pallas kernels  45.3 us (92%)
  other arithmetic  1.61 us (3%)
  between operations  1.29 us (3%)
  local copies, waits for them, and re-layouts  0.66 us (1%)
    pallas_call x1, Pallas kernels, fused(): pl.pallas_call(functools.partial(kernel, n_row, n_col, float(size * n_row...  45.3 us
    convert_element_type x1, other arithmetic, body(): return (hidden, grad.astype(jnp.float32))  1.61 us

profile of v7, /device:TPU:0, one launch (start us, length us, event | category | flops | bytes accessed | tf_op | source)
XLA Modules:
  0.0 48.8 jit_solution(421935963842125503)
XLA Ops:
  1.3 45.3 %shard_map.86 = (bf16[128,512]{1,0:T(8,128)(2,1)S(1)}, bf16[1024,512]{1,0:T(8,128)(2,1)S(1)}) custom-call(bf16[128,512]{1,0:T(8,128)(2,1)} %features.1, bf16[8,128,128]{2,1,0:T(8,128)(2,1)} %bitcast.1, s32[1,8]{1,0:T(1,128)} %rows.1, s32[1,8]{1,0:T(1,128)} %cols.1, s32[1,1]{1,0:T(1,128)S(6)} %copy.11.count, bf16[1024,512]{1,0:T(8,128)(2,1)} %weight_in.1, ...), custom_call_target="tpu_custom_call" | custom-call | tf_op jit(solution)/shard_map/pallas_call | solution.py:270
  46.6 0.7 %copy.10 = bf16[128,512]{1,0:T(8,128)(2,1)} copy(bf16[128,512]{1,0:T(8,128)(2,1)S(1)} %get-tuple-element.6) | data formatting | bytes 262144
  47.2 1.6 %convert_element_type.3 = f32[1024,512]{1,0:T(8,128)} convert(bf16[1024,512]{1,0:T(8,128)(2,1)S(1)} %get-tuple-element.5) | non-fusion elementwise | flops 524288 | bytes 3145728 | tf_op jit(solution)/shard_map/convert_element_type | solution.py:328

commit v8 on v7

--- a/solution.py
+++ b/solution.py
@@ -26,7 +26,7 @@
 
 
 MESH = pl.DeviceIdType.MESH
-PARTS = 4
+PARTS = 2
 
 
 def flip(index, bits):
@@ -85,7 +85,7 @@
         gathers.append([])
         for d in range(1, n_row):
             out, into = copy(features.at[:, columns(p)], slabs[p].at[r],
-                             slabs[p].at[lax.rem(r + n_row - d, n_row)], (lax.rem(r + d, n_row), c))
+                             slabs[p].at[flip(r, n_row - d)], (flip(r, n_row - d), c))
             start(out)
             gathers[p].append(into)
 
@@ -145,6 +145,8 @@
 
     lefts = []
     for p in range(PARTS):
+        if p > 0:
+            place_sibling(p - 1)
         total = own_part[p]
         for k, into in enumerate(sums[p]):
             into.wait_recv()
@@ -159,8 +161,6 @@
             below = weight[width + p * wide:width + (p + 1) * wide]
             self_part[...] += dot(high, below) + dot(low, below)
             place_own(p, high, low)
-            if p > 0:
-                place_sibling(p - 1)
 
     ups = []
     for p in range(PARTS):
@@ -175,8 +175,7 @@
         ups.append(into)
         hidden[:, at] = (pre_act * gate).astype(jnp.bfloat16)
     place_own(PARTS - 1, high, low)
-    for p in range(PARTS - 2, PARTS):
-        place_sibling(p)
+    place_sibling(PARTS - 1)
     for into in ups:
         into.wait_recv()
     upstream = jnp.concatenate([up_give[...], up_taken[...]], axis=0)
@@ -189,7 +188,7 @@
         term[i] = value.astype(jnp.bfloat16)
         over_row.append([])
         for e in range(1, n_row):
-            q = lax.rem(r + e, n_row)
+            q = flip(r, n_row - e)
             at = pl.ds(pl.multiple_of(q * small, small), small)
             out, into = copy(term.at[i, at], term_in.at[i, e - 1], term_in.at[i, e - 1], (q, c))
             start(out)
@@ -240,9 +239,9 @@
         if d > 0:
             back_z[d - 1].wait_recv()
         for e in range(1, n_row):
-            q = lax.rem(r + n_row - e, n_row)
+            q = flip(r, n_row - e)
             out, into = copy(block(core, r, level), block(core, r, level), block(core, q, level),
-                             (lax.rem(r + e, n_row), c))
+                             (q, c))
             start(out)
             back_row.append((q, level, into))
         pass_on(r, level)
@@ -319,7 +318,7 @@
     tiles = adj_tiles[0]
     slots, size = tiles.shape[:2]
     share = width // row_count
-    flippable = col_count // 2 in (4, 8, 16, 32)
+    flippable = col_count // 2 in (4, 8, 16, 32) and row_count in (2, 4, 8, 16)
     small = share // (col_count // 2)
     if REACH == 4 and col_count % 2 == 0 and flippable and small >= 16 and small % 16 == 0:
         hidden, grad = fused(

time: 49 us -> 46.7 us (0.953)
  Pallas kernels: 45.3 us -> 43 us
    pallas_call x1, Pallas kernels: 45.3 us -> 43 us  [fused(): pl.pallas_call(functools.partial(kernel, n_row, n_col, float(size * n_row...]
where the time goes in v8:
time: 46.7 us; the launch traced here: 46.5 us
  Pallas kernels  43 us (92%)
  other arithmetic  1.61 us (3%)
  between operations  1.29 us (3%)
  local copies, waits for them, and re-layouts  0.66 us (1%)
    pallas_call x1, Pallas kernels, fused(): pl.pallas_call(functools.partial(kernel, n_row, n_col, float(size * n_row...  43 us
    convert_element_type x1, other arithmetic, body(): return (hidden, grad.astype(jnp.float32))  1.61 us

profile of v8, /device:TPU:0, one launch (start us, length us, event | category | flops | bytes accessed | tf_op | source)
XLA Modules:
  0.0 46.5 jit_solution(17755250827375055387)
XLA Ops:
  1.3 43.0 %shard_map.86 = (bf16[128,512]{1,0:T(8,128)(2,1)S(1)}, bf16[1024,512]{1,0:T(8,128)(2,1)S(1)}) custom-call(bf16[128,512]{1,0:T(8,128)(2,1)} %features.1, bf16[8,128,128]{2,1,0:T(8,128)(2,1)} %bitcast.1, s32[1,8]{1,0:T(1,128)} %rows.1, s32[1,8]{1,0:T(1,128)} %cols.1, s32[1,1]{1,0:T(1,128)S(6)} %copy.11.count, bf16[1024,512]{1,0:T(8,128)(2,1)} %weight_in.1, ...), custom_call_target="tpu_custom_call" | custom-call | tf_op jit(solution)/shard_map/pallas_call | solution.py:269
  44.3 0.7 %copy.10 = bf16[128,512]{1,0:T(8,128)(2,1)} copy(bf16[128,512]{1,0:T(8,128)(2,1)S(1)} %get-tuple-element.6) | data formatting | bytes 262144
  44.9 1.6 %convert_element_type.3 = f32[1024,512]{1,0:T(8,128)} convert(bf16[1024,512]{1,0:T(8,128)(2,1)S(1)} %get-tuple-element.5) | non-fusion elementwise | flops 524288 | bytes 3145728 | tf_op jit(solution)/shard_map/convert_element_type | solution.py:327

commit v9 on v8

--- a/solution.py
+++ b/solution.py
@@ -110,16 +110,16 @@
             into.wait_recv()
         for s in range(slots):
             chosen[p, s * size:(s + 1) * size, :] = slabs[p][cols[0, s]]
+        swap[p] = dot(masked[3 - 2 * core], chosen[p])
+        out, joining = copy(swap.at[p], swap_in.at[p], swap_in.at[p], sibling)
+        start(out)
         part[p, 0] = dot(masked[1 + 2 * core], chosen[p]).astype(jnp.bfloat16)
         out, straight = copy(part.at[p, 0], arrived.at[p, 0], arrived.at[p, 0],
                              (r, lax.rem(c + 1 + 2 * core, n_col)))
         start(out)
-        swap[p] = dot(masked[3 - 2 * core], chosen[p])
-        out, into = copy(swap.at[p], swap_in.at[p], swap_in.at[p], sibling)
-        start(out)
         joined = dot(masked[2], chosen[p])
         own_part[p] = dot(masked[0], chosen[p])
-        into.wait_recv()
+        joining.wait_recv()
         part[p, 1] = (joined + swap_in[p]).astype(jnp.bfloat16)
         out, into = copy(part.at[p, 1], arrived.at[p, 1], arrived.at[p, 1], (r, lax.rem(c + 2, n_col)))
         start(out)
@@ -310,6 +310,38 @@
     )(features, tiles, rows, cols, count, weight, cotangent)
 
 
+CHUNKS = 8
+
+
+def write_out(hidden, grad, hidden_out, grad_out, wide_grad, sems):
+    moves = [pltpu.make_async_copy(hidden, hidden_out, sems.at[CHUNKS])]
+    moves[0].start()
+    rows = grad.shape[0] // CHUNKS
+    for i in range(CHUNKS):
+        at = pl.ds(i * rows, rows)
+        wide_grad[at] = grad[at].astype(jnp.float32)
+        moves.append(pltpu.make_async_copy(wide_grad.at[at], grad_out.at[at], sems.at[i]))
+        moves[-1].start()
+    for moved in moves:
+        moved.wait()
+
+
+def written(hidden, grad):
+    vmem = pl.BlockSpec(memory_space=pltpu.VMEM)
+    hbm = pl.BlockSpec(memory_space=pl.ANY)
+    return pl.pallas_call(
+        write_out,
+        out_shape=(
+            jax.ShapeDtypeStruct(hidden.shape, hidden.dtype),
+            jax.ShapeDtypeStruct(grad.shape, jnp.float32),
+        ),
+        in_specs=[vmem, vmem],
+        out_specs=(hbm, hbm),
+        scratch_shapes=[pltpu.VMEM(grad.shape, jnp.float32), pltpu.SemaphoreType.DMA((CHUNKS + 1,))],
+        compiler_params=pltpu.CompilerParams(vmem_limit_bytes=40 * 1024 * 1024),
+    )(hidden, grad)
+
+
 def body(features, adj_tiles, tile_rows, tile_cols, tile_count, weight, cotangent):
     width = features.shape[1]
     own_nodes = features.shape[0]
@@ -324,7 +356,7 @@
         hidden, grad = fused(
             features, tiles, tile_rows, tile_cols, tile_count, weight, cotangent, row_count, col_count
         )
-        return hidden, grad.astype(jnp.float32)
+        return written(hidden, grad)
     position = lax.axis_index("col")
     offsets = (tile_rows[0] - position) % col_count
     live = jnp.arange(slots) < tile_count[0, 0]

time: 46.7 us -> 46 us (0.985)
  other arithmetic: 1.61 us -> 0 us
  Pallas kernels: 43 us -> 44.6 us
  local copies, waits for them, and re-layouts: 0.66 us -> 0 us
    convert_element_type x1 -> x0, other arithmetic: 1.61 us -> none  [body(): return (hidden, grad.astype(jnp.float32))]
    pallas_call x0 -> x1, Pallas kernels: none -> 1.43 us  [written(): pl.pallas_call(write_out, out_shape=(jax.ShapeDtypeStruct(hidden.shape, h...]
    unnamed x1 -> x0, local copies, waits for them, and re-layouts: 0.66 us -> none
where the time goes in v9:
time: 46 us; the launch traced here: 45.9 us
  Pallas kernels  44.6 us (97%)
  between operations  1.29 us (3%)
    pallas_call x1, Pallas kernels, fused(): pl.pallas_call(functools.partial(kernel, n_row, n_col, float(size * n_row...  43.1 us
    pallas_call x1, Pallas kernels, written(): pl.pallas_call(write_out, out_shape=(jax.ShapeDtypeStruct(hidden.shape, h...  1.43 us

profile of v9, /device:TPU:0, one launch (start us, length us, event | category | flops | bytes accessed | tf_op | source)
XLA Modules:
  0.0 45.9 jit_solution(16263607508141004425)
XLA Ops:
  1.3 43.1 %shard_map.86 = (bf16[128,512]{1,0:T(8,128)(2,1)S(1)}, bf16[1024,512]{1,0:T(8,128)(2,1)S(1)}) custom-call(bf16[128,512]{1,0:T(8,128)(2,1)} %features.1, bf16[8,128,128]{2,1,0:T(8,128)(2,1)} %bitcast.1, s32[1,8]{1,0:T(1,128)} %rows.1, s32[1,8]{1,0:T(1,128)} %cols.1, s32[1,1]{1,0:T(1,128)S(6)} %copy.9.count, bf16[1024,512]{1,0:T(8,128)(2,1)} %weight_in.1, ...), custom_call_target="tpu_custom_call" | custom-call | tf_op jit(solution)/shard_map/pallas_call | solution.py:269
  44.4 1.4 %shard_map.87 = (bf16[128,512]{1,0:T(8,128)(2,1)}, f32[1024,512]{1,0:T(8,128)}) custom-call(bf16[128,512]{1,0:T(8,128)(2,1)S(1)} %get-tuple-element.4.hidden, bf16[1024,512]{1,0:T(8,128)(2,1)S(1)} %get-tuple-element.5.grad), custom_call_target="tpu_custom_call" | custom-call | tf_op jit(solution)/shard_map/pallas_call | solution.py:332
